TPU v7x, 32 devices: a whole 2x2x4 slice. The times are simulated.
32 devices in a mesh: blk: 16 (over z, y, core), lag: 2 (over x).
Axes of the slice: x: 2, y: 2, z: 4, core: 2. Of those that a mesh axis runs over, the one named last changes fastest.
Arguments:
- spectra: bfloat16 [2048, 3, 2, 1024], P('blk', None, None, 'lag'), may hold values from -6 to 6
- band: int32 [2048, 2], P('blk'), may hold values from 0 to 1024, as said below
- pair_lists: int32 [16, 9, 96, 2], P('blk'), may hold values from 0 to 127
- pair_counts: int32 [16, 9], P('blk'), may hold values from 32 to 96, as said below
Outputs:
- gradient: float32 [2048, 3, 2, 1024], P('blk', None, None, 'lag')
Inputs may be any that keep to these rules, and one draw needn't show every extreme that they name: band[s, 0] < band[s, 1]; band[s, 0] is at most 128 and band[s, 1] at least 896; some station starts at 0 and some ends at 1024. `pair_counts`: at least a third of the slots are used; in every block one offset uses all 96 slots.
All inputs are finite; a program needn't handle non-finite values.
Results may differ from a plain program's by a relative error of at most 0.0045.
Values may be sent and summed in bfloat16 or wider, within the bound.
A program may use at most 64 MiB of HBM per device.

v0:
```python
import math

import jax
import jax.numpy as jnp
from jax import lax
from jax.sharding import PartitionSpec as P


def from_behind(block, axis, distance):
    devices = range(lax.axis_size(axis))
    route = [((i - distance) % len(devices), i) for i in devices]
    return lax.ppermute(block, axis, route)


def phase_table(freq_ids, lag_ids, lag_total, freq_total):
    turns = freq_ids[:, None] * lag_ids[None, :] % lag_total
    angle = turns.astype(jnp.float32) * (2.0 * jnp.pi / lag_total)
    factor = 1.0 / jnp.sqrt(jnp.float32(freq_total))
    return jnp.stack([jnp.cos(angle) * factor, -jnp.sin(angle) * factor], 0).astype(jnp.bfloat16)


def whiten(spectra, band, freq_ids):
    values = spectra.astype(jnp.float32)
    meansq = jnp.mean(values * values, axis=(1, 2))
    inside = (freq_ids[None, :] >= band[:, 0:1]) & (freq_ids[None, :] < band[:, 1:2])
    factor = jnp.where(inside, 1.0 / jnp.sqrt(jnp.maximum(meansq, 0.25)), 0.0)
    return (values * factor[:, None, None, :]).astype(jnp.bfloat16)


def on_device(spectra, band, pair_lists, pair_counts):
    stations, comps, parts, bins_local = spectra.shape
    slots = pair_lists.shape[2]
    steps = pair_lists.shape[1]
    lanes = lax.axis_size("lag")
    freq_total = bins_local * lanes
    lag_total = 2 * freq_total
    lag_local = lag_total // lanes
    width = comps * parts * bins_local
    lane = lax.axis_index("lag")
    freq_ids = lane * bins_local + jnp.arange(bins_local, dtype=jnp.int32)
    lag_ids = lane * lag_local + jnp.arange(lag_local, dtype=jnp.int32)
    resident = whiten(spectra, band, freq_ids)
    local_table = phase_table(
        freq_ids, jnp.arange(lag_total, dtype=jnp.int32), lag_total, freq_total
    )
    weight = 1.0 + 3.0 * lag_ids.astype(jnp.float32) / lag_total
    station_ids = jnp.arange(stations, dtype=jnp.int32)
    slot_ids = jnp.arange(slots, dtype=jnp.int32)

    def forward(cross):
        return lax.psum_scatter(
            jnp.einsum("prf,rft->tp", cross, local_table, preferred_element_type=jnp.float32),
            "lag",
            scatter_dimension=0,
            tiled=True,
        ).T

    def back(piece):
        return jnp.einsum("pt,rft->prf", piece, local_table, preferred_element_type=jnp.float32)

    def correlate(arriving, pairs, count):
        first = pairs[:, 0]
        second = pairs[:, 1]
        pick_first = (first[:, None] == station_ids[None, :]).astype(jnp.bfloat16)
        pick_second = (second[:, None] == station_ids[None, :]).astype(jnp.bfloat16)
        rows_a = jnp.dot(
            pick_first, resident.reshape(stations, width), preferred_element_type=jnp.float32
        )
        rows_b = jnp.dot(
            pick_second, arriving.reshape(stations, width), preferred_element_type=jnp.float32
        )
        rows_a = rows_a.reshape(slots, comps, parts, bins_local)
        rows_b = rows_b.reshape(slots, comps, parts, bins_local)
        real_a, imag_a = (rows_a[:, :, 0], rows_a[:, :, 1])
        real_b, imag_b = (rows_b[:, :, 0], rows_b[:, :, 1])
        valid = (slot_ids < count).astype(jnp.float32)[:, None]
        cross_real = jnp.sum(real_a * real_b + imag_a * imag_b, axis=1) * valid
        cross_imag = jnp.sum(imag_a * real_b - real_a * imag_b, axis=1) * valid
        cross = jnp.stack([cross_real, cross_imag], 1).astype(jnp.bfloat16)
        lagged = forward(cross)
        energy = lax.psum(jnp.sum(weight[None, :] * lagged * lagged, axis=1) / lag_total, "lag")
        adjoint = (weight[None, :] * lagged / jnp.sqrt(energy + 1e-05)[:, None]).astype(
            jnp.bfloat16
        )
        spectral = back(lax.all_gather(adjoint, "lag", axis=1, tiled=True))
        adj_real = spectral[:, None, 0]
        adj_imag = spectral[:, None, 1]
        near = jnp.stack(
            [adj_real * real_b - adj_imag * imag_b, adj_real * imag_b + adj_imag * real_b], 2
        )
        far = jnp.stack(
            [adj_real * real_a + adj_imag * imag_a, adj_real * imag_a - adj_imag * real_a], 2
        )
        near = near.astype(jnp.bfloat16).reshape(slots, width)
        far = far.astype(jnp.bfloat16).reshape(slots, width)
        own = jnp.einsum("ps,pw->sw", pick_first, near, preferred_element_type=jnp.float32)
        return (own, far, second, pick_second)

    def visit(step, arriving, total, carried):
        own, far, second, pick_second = correlate(
            arriving, pair_lists[0, step], pair_counts[0, step]
        )
        total = total + own
        carried = carried + jnp.einsum(
            "ps,pw->sw", pick_second, far, preferred_element_type=jnp.float32
        )
        return (total, carried)

    def advance(step, state):
        arriving, total, carried = state
        arriving = from_behind(arriving, "blk", 1)
        carried = from_behind(carried, "blk", 1)
        total, carried = visit(step, arriving, total, carried)
        return (arriving, total, carried)

    start_carried = jnp.zeros((stations, width), jnp.float32)
    total, carried = visit(0, resident, jnp.zeros((stations, width), jnp.float32), start_carried)
    arriving, total, carried = lax.fori_loop(1, steps, advance, (resident, total, carried))
    total = total + from_behind(carried, "blk", -(steps - 1))
    gradient = total / math.sqrt(slots)
    return gradient.reshape(stations, comps, parts, bins_local)


def solution(mesh):
    in_specs = (
        P("blk", None, None, "lag"),
        P("blk", None),
        P("blk", None, None, None),
        P("blk", None),
    )
    out_specs = P("blk", None, None, "lag")
    return jax.shard_map(
        on_device, mesh=mesh, in_specs=in_specs, out_specs=out_specs, check_vma=False
    )
```

profile of v0, /device:TPU:0, one launch (start us, length us, event | category | flops | bytes accessed | tf_op | source)
XLA Modules:
  0.0 632.1 jit_solution(2502336810722881425)
XLA Ops:
  11.1 18.2 %multiply_convert_fusion.1 = (bf16[1,512,2048]{2,1,0:T(8,128)(2,1)S(1)}, bf16[1,512,2048]{2,1,0:T(8,128)(2,1)S(1)}) fusion(s32[512]{0:T(512)S(1)} %iota_add_fusion), kind=kLoop, calls=%fused_computation.58 | loop fusion | flops 19922944 | bytes 4196352 | tf_op jit(solution)/shard_map/convert.12
  39.3 14.8 %reduce-scatter.3.cloned.1.call-done = f32[1024,96]{0,1:T(8,128)} async-done(((f32[2048,96]{0,1:T(8,128)}), f32[1024,96]{0,1:T(8,128)}) %reduce-scatter.3.cloned.1.call-update) | async-done | bytes 393232 | tf_op jit(solution)/shard_map/reduce_scatter | solution.py:51
  55.3 4.9 psum.21
  61.4 6.3 %all_gather.13 = bf16[96,2048]{1,0:T(8,128)(2,1)S(1)} all-gather(bf16[96,1024]{1,0:T(8,128)(2,1)S(1)} %fusion.41), channel_id=1, replica_groups=mesh['blk'=16,'lag'=2] {'lag'}, dimensions={1}, use_global_device_ids=true | all-gather | bytes 589824 | tf_op jit(solution)/shard_map/all_gather | solution.py:85
  77.5 474.7 %while.21 = (s32[]{:T(128)}, bf16[128,3,2,512]{0,3,2,1:T(8,128)(2,1)}, f32[128,3072]{1,0:T(8,128)}, f32[128,3072]{1,0:T(8,128)}, s32[1,9,96,2]{2,3,1,0:T(2,128)}...) while((s32[]{:T(128)}, ...), condition=%wide.region_12.13_spmd.clone.clone, body=%wide.region_6.12_spmd.clone.clone.sunk | while | flops 1113051648 | bytes 88494768 | solution.py:118
  80.1 11.7 %collective-permute-done = bf16[128,3,2,512]{0,3,2,1:T(8,128)(2,1)S(1)} collective-permute-done((bf16[128,3,2,512]{0,3,2,1:T(8,128)(2,1)}, bf16[128,3,2,512]{0,3,2,1:T(8,128)(2,1)S(1)}, u32[]{:S(2)}, u32[]{:S(2)}) %collective-permute-start) | collective-permute-done | bytes 786464 | tf_op jit(solution)/shard_map/while/body/eval_jaxpr/ppermute | solution.py:12
  96.8 13.9 %reduce-scatter.5.cloned.1.call-done = f32[1024,96]{0,1:T(8,128)} async-done(((f32[2048,96]{0,1:T(8,128)}), f32[1024,96]{0,1:T(8,128)}) %reduce-scatter.5.cloned.1.call-update) | async-done | bytes 393232 | tf_op jit(solution)/shard_map/while/body/eval_jaxpr/reduce_scatter | solution.py:51
  111.8 4.9 psum.25
  117.8 6.6 %all_gather.17 = bf16[96,2048]{1,0:T(8,128)(2,1)S(1)} all-gather(bf16[96,1024]{1,0:T(8,128)(2,1)S(1)} %fusion.96), channel_id=1, replica_groups=mesh['blk'=16,'lag'=2] {'lag'}, dimensions={1}, use_global_device_ids=true | all-gather | bytes 589824 | tf_op jit(solution)/shard_map/while/body/eval_jaxpr/all_gather | solution.py:85
  139.6 11.8 %collective-permute-done = bf16[128,3,2,512]{0,3,2,1:T(8,128)(2,1)S(1)} collective-permute-done((bf16[128,3,2,512]{0,3,2,1:T(8,128)(2,1)}, bf16[128,3,2,512]{0,3,2,1:T(8,128)(2,1)S(1)}, u32[]{:S(2)}, u32[]{:S(2)}) %collective-permute-start) | collective-permute-done | bytes 786464 | tf_op jit(solution)/shard_map/while/body/eval_jaxpr/ppermute | solution.py:12
  156.3 13.7 %reduce-scatter.5.cloned.1.call-done = f32[1024,96]{0,1:T(8,128)} async-done(((f32[2048,96]{0,1:T(8,128)}), f32[1024,96]{0,1:T(8,128)}) %reduce-scatter.5.cloned.1.call-update) | async-done | bytes 393232 | tf_op jit(solution)/shard_map/while/body/eval_jaxpr/reduce_scatter | solution.py:51
  177.2 6.6 %all_gather.17 = bf16[96,2048]{1,0:T(8,128)(2,1)S(1)} all-gather(bf16[96,1024]{1,0:T(8,128)(2,1)S(1)} %fusion.96), channel_id=1, replica_groups=mesh['blk'=16,'lag'=2] {'lag'}, dimensions={1}, use_global_device_ids=true | all-gather | bytes 589824 | tf_op jit(solution)/shard_map/while/body/eval_jaxpr/all_gather | solution.py:85
  198.9 11.8 %collective-permute-done = bf16[128,3,2,512]{0,3,2,1:T(8,128)(2,1)S(1)} collective-permute-done((bf16[128,3,2,512]{0,3,2,1:T(8,128)(2,1)}, bf16[128,3,2,512]{0,3,2,1:T(8,128)(2,1)S(1)}, u32[]{:S(2)}, u32[]{:S(2)}) %collective-permute-start) | collective-permute-done | bytes 786464 | tf_op jit(solution)/shard_map/while/body/eval_jaxpr/ppermute | solution.py:12
  215.6 13.6 %reduce-scatter.5.cloned.1.call-done = f32[1024,96]{0,1:T(8,128)} async-done(((f32[2048,96]{0,1:T(8,128)}), f32[1024,96]{0,1:T(8,128)}) %reduce-scatter.5.cloned.1.call-update) | async-done | bytes 393232 | tf_op jit(solution)/shard_map/while/body/eval_jaxpr/reduce_scatter | solution.py:51
  236.5 6.6 %all_gather.17 = bf16[96,2048]{1,0:T(8,128)(2,1)S(1)} all-gather(bf16[96,1024]{1,0:T(8,128)(2,1)S(1)} %fusion.96), channel_id=1, replica_groups=mesh['blk'=16,'lag'=2] {'lag'}, dimensions={1}, use_global_device_ids=true | all-gather | bytes 589824 | tf_op jit(solution)/shard_map/while/body/eval_jaxpr/all_gather | solution.py:85
  258.2 11.8 %collective-permute-done = bf16[128,3,2,512]{0,3,2,1:T(8,128)(2,1)S(1)} collective-permute-done((bf16[128,3,2,512]{0,3,2,1:T(8,128)(2,1)}, bf16[128,3,2,512]{0,3,2,1:T(8,128)(2,1)S(1)}, u32[]{:S(2)}, u32[]{:S(2)}) %collective-permute-start) | collective-permute-done | bytes 786464 | tf_op jit(solution)/shard_map/while/body/eval_jaxpr/ppermute | solution.py:12
  274.9 13.6 %reduce-scatter.5.cloned.1.call-done = f32[1024,96]{0,1:T(8,128)} async-done(((f32[2048,96]{0,1:T(8,128)}), f32[1024,96]{0,1:T(8,128)}) %reduce-scatter.5.cloned.1.call-update) | async-done | bytes 393232 | tf_op jit(solution)/shard_map/while/body/eval_jaxpr/reduce_scatter | solution.py:51
  295.8 6.6 %all_gather.17 = bf16[96,2048]{1,0:T(8,128)(2,1)S(1)} all-gather(bf16[96,1024]{1,0:T(8,128)(2,1)S(1)} %fusion.96), channel_id=1, replica_groups=mesh['blk'=16,'lag'=2] {'lag'}, dimensions={1}, use_global_device_ids=true | all-gather | bytes 589824 | tf_op jit(solution)/shard_map/while/body/eval_jaxpr/all_gather | solution.py:85
  317.5 11.8 %collective-permute-done = bf16[128,3,2,512]{0,3,2,1:T(8,128)(2,1)S(1)} collective-permute-done((bf16[128,3,2,512]{0,3,2,1:T(8,128)(2,1)}, bf16[128,3,2,512]{0,3,2,1:T(8,128)(2,1)S(1)}, u32[]{:S(2)}, u32[]{:S(2)}) %collective-permute-start) | collective-permute-done | bytes 786464 | tf_op jit(solution)/shard_map/while/body/eval_jaxpr/ppermute | solution.py:12
  334.2 13.7 %reduce-scatter.5.cloned.1.call-done = f32[1024,96]{0,1:T(8,128)} async-done(((f32[2048,96]{0,1:T(8,128)}), f32[1024,96]{0,1:T(8,128)}) %reduce-scatter.5.cloned.1.call-update) | async-done | bytes 393232 | tf_op jit(solution)/shard_map/while/body/eval_jaxpr/reduce_scatter | solution.py:51
  355.1 6.6 %all_gather.17 = bf16[96,2048]{1,0:T(8,128)(2,1)S(1)} all-gather(bf16[96,1024]{1,0:T(8,128)(2,1)S(1)} %fusion.96), channel_id=1, replica_groups=mesh['blk'=16,'lag'=2] {'lag'}, dimensions={1}, use_global_device_ids=true | all-gather | bytes 589824 | tf_op jit(solution)/shard_map/while/body/eval_jaxpr/all_gather | solution.py:85
  376.8 11.8 %collective-permute-done = bf16[128,3,2,512]{0,3,2,1:T(8,128)(2,1)S(1)} collective-permute-done((bf16[128,3,2,512]{0,3,2,1:T(8,128)(2,1)}, bf16[128,3,2,512]{0,3,2,1:T(8,128)(2,1)S(1)}, u32[]{:S(2)}, u32[]{:S(2)}) %collective-permute-start) | collective-permute-done | bytes 786464 | tf_op jit(solution)/shard_map/while/body/eval_jaxpr/ppermute | solution.py:12
  393.5 13.7 %reduce-scatter.5.cloned.1.call-done = f32[1024,96]{0,1:T(8,128)} async-done(((f32[2048,96]{0,1:T(8,128)}), f32[1024,96]{0,1:T(8,128)}) %reduce-scatter.5.cloned.1.call-update) | async-done | bytes 393232 | tf_op jit(solution)/shard_map/while/body/eval_jaxpr/reduce_scatter | solution.py:51
  414.4 6.6 %all_gather.17 = bf16[96,2048]{1,0:T(8,128)(2,1)S(1)} all-gather(bf16[96,1024]{1,0:T(8,128)(2,1)S(1)} %fusion.96), channel_id=1, replica_groups=mesh['blk'=16,'lag'=2] {'lag'}, dimensions={1}, use_global_device_ids=true | all-gather | bytes 589824 | tf_op jit(solution)/shard_map/while/body/eval_jaxpr/all_gather | solution.py:85
  436.2 11.8 %collective-permute-done = bf16[128,3,2,512]{0,3,2,1:T(8,128)(2,1)S(1)} collective-permute-done((bf16[128,3,2,512]{0,3,2,1:T(8,128)(2,1)}, bf16[128,3,2,512]{0,3,2,1:T(8,128)(2,1)S(1)}, u32[]{:S(2)}, u32[]{:S(2)}) %collective-permute-start) | collective-permute-done | bytes 786464 | tf_op jit(solution)/shard_map/while/body/eval_jaxpr/ppermute | solution.py:12
  452.9 13.7 %reduce-scatter.5.cloned.1.call-done = f32[1024,96]{0,1:T(8,128)} async-done(((f32[2048,96]{0,1:T(8,128)}), f32[1024,96]{0,1:T(8,128)}) %reduce-scatter.5.cloned.1.call-update) | async-done | bytes 393232 | tf_op jit(solution)/shard_map/while/body/eval_jaxpr/reduce_scatter | solution.py:51
  473.7 6.6 %all_gather.17 = bf16[96,2048]{1,0:T(8,128)(2,1)S(1)} all-gather(bf16[96,1024]{1,0:T(8,128)(2,1)S(1)} %fusion.96), channel_id=1, replica_groups=mesh['blk'=16,'lag'=2] {'lag'}, dimensions={1}, use_global_device_ids=true | all-gather | bytes 589824 | tf_op jit(solution)/shard_map/while/body/eval_jaxpr/all_gather | solution.py:85
  495.5 11.8 %collective-permute-done = bf16[128,3,2,512]{0,3,2,1:T(8,128)(2,1)S(1)} collective-permute-done((bf16[128,3,2,512]{0,3,2,1:T(8,128)(2,1)}, bf16[128,3,2,512]{0,3,2,1:T(8,128)(2,1)S(1)}, u32[]{:S(2)}, u32[]{:S(2)}) %collective-permute-start) | collective-permute-done | bytes 786464 | tf_op jit(solution)/shard_map/while/body/eval_jaxpr/ppermute | solution.py:12
  512.2 13.7 %reduce-scatter.5.cloned.1.call-done = f32[1024,96]{0,1:T(8,128)} async-done(((f32[2048,96]{0,1:T(8,128)}), f32[1024,96]{0,1:T(8,128)}) %reduce-scatter.5.cloned.1.call-update) | async-done | bytes 393232 | tf_op jit(solution)/shard_map/while/body/eval_jaxpr/reduce_scatter | solution.py:51
  527.0 4.9 psum.25
  533.1 6.6 %all_gather.17 = bf16[96,2048]{1,0:T(8,128)(2,1)S(1)} all-gather(bf16[96,1024]{1,0:T(8,128)(2,1)S(1)} %fusion.96), channel_id=1, replica_groups=mesh['blk'=16,'lag'=2] {'lag'}, dimensions={1}, use_global_device_ids=true | all-gather | bytes 589824 | tf_op jit(solution)/shard_map/while/body/eval_jaxpr/all_gather | solution.py:85
  554.3 67.1 %collective-permute-done.2 = f32[128,3072]{1,0:T(8,128)S(1)} collective-permute-done((f32[128,3072]{1,0:T(8,128)}, f32[128,3072]{1,0:T(8,128)S(1)}, u32[]{:S(2)}, u32[]{:S(2)}) %collective-permute-start.2) | collective-permute-done | bytes 1572896 | tf_op jit(solution)/shard_map/ppermute | solution.py:12
  (372 shorter events, 240.0 us)
Async XLA Ops:
  6.5 47.6 %reduce-scatter.3.cloned.1.call-start = ((), (), s32[]{:S(2)}) async-start(), calls=%async_computation.2 | async-start | bytes 1179648 | tf_op jit(solution)/shard_map/reduce_scatter | solution.py:51
  77.5 33.2 %reduce-scatter.5.cloned.1.call-start = ((), (), s32[]{:S(2)}) async-start(), calls=%async_computation.3 | async-start | bytes 1179648 | tf_op jit(solution)/shard_map/while/body/eval_jaxpr/reduce_scatter | solution.py:51
  77.5 14.4 %collective-permute-start = (bf16[128,3,2,512]{0,3,2,1:T(8,128)(2,1)}, bf16[128,3,2,512]{0,3,2,1:T(8,128)(2,1)S(1)}, u32[]{:S(2)}, u32[]{:S(2)}) collective-permute-start(bf16[128,3,2,512]{0,3,2,1:T(8,128)(2,1)} %get-tuple-element.474), channel_id=1, source_target_pairs={{30,0},{0,2},{2,4},{4,6},{6,8},{8,10},{10,12},{12,14},{14,16},{16,... | collective-permute-start | bytes 2359304 | tf_op jit(solution)/shard_map/while/body/eval_jaxpr/ppermute | solution.py:12
  95.8 37.5 %collective-permute-start.1 = (f32[128,3072]{1,0:T(8,128)}, f32[128,3072]{1,0:T(8,128)}, u32[]{:S(2)}, u32[]{:S(2)}) collective-permute-start(f32[128,3072]{1,0:T(8,128)} %get-tuple-element.476), channel_id=1, source_target_pairs={{30,0},{0,2},{2,4},{4,6},{6,8},{8,10},{10,12},{12,14},{14,16},{16,... | collective-permute-start | bytes 4718600 | tf_op jit(solution)/shard_map/while/body/eval_jaxpr/ppermute | solution.py:12
  136.9 14.4 %copy-start.3 = (bf16[128,3,2,512]{0,3,2,1:T(8,128)(2,1)}, bf16[128,3,2,512]{0,3,2,1:T(8,128)(2,1)S(1)}, u32[]{:S(2)}) copy-start(bf16[128,3,2,512]{0,3,2,1:T(8,128)(2,1)S(1)} %get-tuple-element.490) | copy-start | bytes 2359300 | tf_op jit(solution)/shard_map/while
  136.9 33.0 %reduce-scatter.5.cloned.1.call-start = ((), (), s32[]{:S(2)}) async-start(), calls=%async_computation.3 | async-start | bytes 1179648 | tf_op jit(solution)/shard_map/while/body/eval_jaxpr/reduce_scatter | solution.py:51
  137.0 14.4 %collective-permute-start = (bf16[128,3,2,512]{0,3,2,1:T(8,128)(2,1)}, bf16[128,3,2,512]{0,3,2,1:T(8,128)(2,1)S(1)}, u32[]{:S(2)}, u32[]{:S(2)}) collective-permute-start(bf16[128,3,2,512]{0,3,2,1:T(8,128)(2,1)} %get-tuple-element.474), channel_id=1, source_target_pairs={{30,0},{0,2},{2,4},{4,6},{6,8},{8,10},{10,12},{12,14},{14,16},{16,... | collective-permute-start | bytes 2359304 | tf_op jit(solution)/shard_map/while/body/eval_jaxpr/ppermute | solution.py:12
  155.3 37.3 %collective-permute-start.1 = (f32[128,3072]{1,0:T(8,128)}, f32[128,3072]{1,0:T(8,128)}, u32[]{:S(2)}, u32[]{:S(2)}) collective-permute-start(f32[128,3072]{1,0:T(8,128)} %get-tuple-element.476), channel_id=1, source_target_pairs={{30,0},{0,2},{2,4},{4,6},{6,8},{8,10},{10,12},{12,14},{14,16},{16,... | collective-permute-start | bytes 4718600 | tf_op jit(solution)/shard_map/while/body/eval_jaxpr/ppermute | solution.py:12
  196.3 14.4 %copy-start.3 = (bf16[128,3,2,512]{0,3,2,1:T(8,128)(2,1)}, bf16[128,3,2,512]{0,3,2,1:T(8,128)(2,1)S(1)}, u32[]{:S(2)}) copy-start(bf16[128,3,2,512]{0,3,2,1:T(8,128)(2,1)S(1)} %get-tuple-element.490) | copy-start | bytes 2359300 | tf_op jit(solution)/shard_map/while
  196.3 33.0 %reduce-scatter.5.cloned.1.call-start = ((), (), s32[]{:S(2)}) async-start(), calls=%async_computation.3 | async-start | bytes 1179648 | tf_op jit(solution)/shard_map/while/body/eval_jaxpr/reduce_scatter | solution.py:51
  196.3 14.4 %collective-permute-start = (bf16[128,3,2,512]{0,3,2,1:T(8,128)(2,1)}, bf16[128,3,2,512]{0,3,2,1:T(8,128)(2,1)S(1)}, u32[]{:S(2)}, u32[]{:S(2)}) collective-permute-start(bf16[128,3,2,512]{0,3,2,1:T(8,128)(2,1)} %get-tuple-element.474), channel_id=1, source_target_pairs={{30,0},{0,2},{2,4},{4,6},{6,8},{8,10},{10,12},{12,14},{14,16},{16,... | collective-permute-start | bytes 2359304 | tf_op jit(solution)/shard_map/while/body/eval_jaxpr/ppermute | solution.py:12
  214.6 37.3 %collective-permute-start.1 = (f32[128,3072]{1,0:T(8,128)}, f32[128,3072]{1,0:T(8,128)}, u32[]{:S(2)}, u32[]{:S(2)}) collective-permute-start(f32[128,3072]{1,0:T(8,128)} %get-tuple-element.476), channel_id=1, source_target_pairs={{30,0},{0,2},{2,4},{4,6},{6,8},{8,10},{10,12},{12,14},{14,16},{16,... | collective-permute-start | bytes 4718600 | tf_op jit(solution)/shard_map/while/body/eval_jaxpr/ppermute | solution.py:12
  255.6 14.4 %copy-start.3 = (bf16[128,3,2,512]{0,3,2,1:T(8,128)(2,1)}, bf16[128,3,2,512]{0,3,2,1:T(8,128)(2,1)S(1)}, u32[]{:S(2)}) copy-start(bf16[128,3,2,512]{0,3,2,1:T(8,128)(2,1)S(1)} %get-tuple-element.490) | copy-start | bytes 2359300 | tf_op jit(solution)/shard_map/while
  255.6 33.0 %reduce-scatter.5.cloned.1.call-start = ((), (), s32[]{:S(2)}) async-start(), calls=%async_computation.3 | async-start | bytes 1179648 | tf_op jit(solution)/shard_map/while/body/eval_jaxpr/reduce_scatter | solution.py:51
  255.6 14.4 %collective-permute-start = (bf16[128,3,2,512]{0,3,2,1:T(8,128)(2,1)}, bf16[128,3,2,512]{0,3,2,1:T(8,128)(2,1)S(1)}, u32[]{:S(2)}, u32[]{:S(2)}) collective-permute-start(bf16[128,3,2,512]{0,3,2,1:T(8,128)(2,1)} %get-tuple-element.474), channel_id=1, source_target_pairs={{30,0},{0,2},{2,4},{4,6},{6,8},{8,10},{10,12},{12,14},{14,16},{16,... | collective-permute-start | bytes 2359304 | tf_op jit(solution)/shard_map/while/body/eval_jaxpr/ppermute | solution.py:12
  273.9 37.3 %collective-permute-start.1 = (f32[128,3072]{1,0:T(8,128)}, f32[128,3072]{1,0:T(8,128)}, u32[]{:S(2)}, u32[]{:S(2)}) collective-permute-start(f32[128,3072]{1,0:T(8,128)} %get-tuple-element.476), channel_id=1, source_target_pairs={{30,0},{0,2},{2,4},{4,6},{6,8},{8,10},{10,12},{12,14},{14,16},{16,... | collective-permute-start | bytes 4718600 | tf_op jit(solution)/shard_map/while/body/eval_jaxpr/ppermute | solution.py:12
  314.9 14.4 %copy-start.3 = (bf16[128,3,2,512]{0,3,2,1:T(8,128)(2,1)}, bf16[128,3,2,512]{0,3,2,1:T(8,128)(2,1)S(1)}, u32[]{:S(2)}) copy-start(bf16[128,3,2,512]{0,3,2,1:T(8,128)(2,1)S(1)} %get-tuple-element.490) | copy-start | bytes 2359300 | tf_op jit(solution)/shard_map/while
  314.9 33.0 %reduce-scatter.5.cloned.1.call-start = ((), (), s32[]{:S(2)}) async-start(), calls=%async_computation.3 | async-start | bytes 1179648 | tf_op jit(solution)/shard_map/while/body/eval_jaxpr/reduce_scatter | solution.py:51
  314.9 14.4 %collective-permute-start = (bf16[128,3,2,512]{0,3,2,1:T(8,128)(2,1)}, bf16[128,3,2,512]{0,3,2,1:T(8,128)(2,1)S(1)}, u32[]{:S(2)}, u32[]{:S(2)}) collective-permute-start(bf16[128,3,2,512]{0,3,2,1:T(8,128)(2,1)} %get-tuple-element.474), channel_id=1, source_target_pairs={{30,0},{0,2},{2,4},{4,6},{6,8},{8,10},{10,12},{12,14},{14,16},{16,... | collective-permute-start | bytes 2359304 | tf_op jit(solution)/shard_map/while/body/eval_jaxpr/ppermute | solution.py:12
  333.2 37.3 %collective-permute-start.1 = (f32[128,3072]{1,0:T(8,128)}, f32[128,3072]{1,0:T(8,128)}, u32[]{:S(2)}, u32[]{:S(2)}) collective-permute-start(f32[128,3072]{1,0:T(8,128)} %get-tuple-element.476), channel_id=1, source_target_pairs={{30,0},{0,2},{2,4},{4,6},{6,8},{8,10},{10,12},{12,14},{14,16},{16,... | collective-permute-start | bytes 4718600 | tf_op jit(solution)/shard_map/while/body/eval_jaxpr/ppermute | solution.py:12
  374.2 14.4 %copy-start.3 = (bf16[128,3,2,512]{0,3,2,1:T(8,128)(2,1)}, bf16[128,3,2,512]{0,3,2,1:T(8,128)(2,1)S(1)}, u32[]{:S(2)}) copy-start(bf16[128,3,2,512]{0,3,2,1:T(8,128)(2,1)S(1)} %get-tuple-element.490) | copy-start | bytes 2359300 | tf_op jit(solution)/shard_map/while
  374.2 33.0 %reduce-scatter.5.cloned.1.call-start = ((), (), s32[]{:S(2)}) async-start(), calls=%async_computation.3 | async-start | bytes 1179648 | tf_op jit(solution)/shard_map/while/body/eval_jaxpr/reduce_scatter | solution.py:51
  374.2 14.4 %collective-permute-start = (bf16[128,3,2,512]{0,3,2,1:T(8,128)(2,1)}, bf16[128,3,2,512]{0,3,2,1:T(8,128)(2,1)S(1)}, u32[]{:S(2)}, u32[]{:S(2)}) collective-permute-start(bf16[128,3,2,512]{0,3,2,1:T(8,128)(2,1)} %get-tuple-element.474), channel_id=1, source_target_pairs={{30,0},{0,2},{2,4},{4,6},{6,8},{8,10},{10,12},{12,14},{14,16},{16,... | collective-permute-start | bytes 2359304 | tf_op jit(solution)/shard_map/while/body/eval_jaxpr/ppermute | solution.py:12
  392.5 37.3 %collective-permute-start.1 = (f32[128,3072]{1,0:T(8,128)}, f32[128,3072]{1,0:T(8,128)}, u32[]{:S(2)}, u32[]{:S(2)}) collective-permute-start(f32[128,3072]{1,0:T(8,128)} %get-tuple-element.476), channel_id=1, source_target_pairs={{30,0},{0,2},{2,4},{4,6},{6,8},{8,10},{10,12},{12,14},{14,16},{16,... | collective-permute-start | bytes 4718600 | tf_op jit(solution)/shard_map/while/body/eval_jaxpr/ppermute | solution.py:12
  433.5 33.0 %reduce-scatter.5.cloned.1.call-start = ((), (), s32[]{:S(2)}) async-start(), calls=%async_computation.3 | async-start | bytes 1179648 | tf_op jit(solution)/shard_map/while/body/eval_jaxpr/reduce_scatter | solution.py:51
  433.6 14.4 %collective-permute-start = (bf16[128,3,2,512]{0,3,2,1:T(8,128)(2,1)}, bf16[128,3,2,512]{0,3,2,1:T(8,128)(2,1)S(1)}, u32[]{:S(2)}, u32[]{:S(2)}) collective-permute-start(bf16[128,3,2,512]{0,3,2,1:T(8,128)(2,1)} %get-tuple-element.474), channel_id=1, source_target_pairs={{30,0},{0,2},{2,4},{4,6},{6,8},{8,10},{10,12},{12,14},{14,16},{16,... | collective-permute-start | bytes 2359304 | tf_op jit(solution)/shard_map/while/body/eval_jaxpr/ppermute | solution.py:12
  451.8 37.3 %collective-permute-start.1 = (f32[128,3072]{1,0:T(8,128)}, f32[128,3072]{1,0:T(8,128)}, u32[]{:S(2)}, u32[]{:S(2)}) collective-permute-start(f32[128,3072]{1,0:T(8,128)} %get-tuple-element.476), channel_id=1, source_target_pairs={{30,0},{0,2},{2,4},{4,6},{6,8},{8,10},{10,12},{12,14},{14,16},{16,... | collective-permute-start | bytes 4718600 | tf_op jit(solution)/shard_map/while/body/eval_jaxpr/ppermute | solution.py:12
  492.8 14.4 %copy-start.3 = (bf16[128,3,2,512]{0,3,2,1:T(8,128)(2,1)}, bf16[128,3,2,512]{0,3,2,1:T(8,128)(2,1)S(1)}, u32[]{:S(2)}) copy-start(bf16[128,3,2,512]{0,3,2,1:T(8,128)(2,1)S(1)} %get-tuple-element.490) | copy-start | bytes 2359300 | tf_op jit(solution)/shard_map/while
  492.8 33.0 %reduce-scatter.5.cloned.1.call-start = ((), (), s32[]{:S(2)}) async-start(), calls=%async_computation.3 | async-start | bytes 1179648 | tf_op jit(solution)/shard_map/while/body/eval_jaxpr/reduce_scatter | solution.py:51
  492.9 14.4 %collective-permute-start = (bf16[128,3,2,512]{0,3,2,1:T(8,128)(2,1)}, bf16[128,3,2,512]{0,3,2,1:T(8,128)(2,1)S(1)}, u32[]{:S(2)}, u32[]{:S(2)}) collective-permute-start(bf16[128,3,2,512]{0,3,2,1:T(8,128)(2,1)} %get-tuple-element.474), channel_id=1, source_target_pairs={{30,0},{0,2},{2,4},{4,6},{6,8},{8,10},{10,12},{12,14},{14,16},{16,... | collective-permute-start | bytes 2359304 | tf_op jit(solution)/shard_map/while/body/eval_jaxpr/ppermute | solution.py:12
  511.2 37.3 %collective-permute-start.1 = (f32[128,3072]{1,0:T(8,128)}, f32[128,3072]{1,0:T(8,128)}, u32[]{:S(2)}, u32[]{:S(2)}) collective-permute-start(f32[128,3072]{1,0:T(8,128)} %get-tuple-element.476), channel_id=1, source_target_pairs={{30,0},{0,2},{2,4},{4,6},{6,8},{8,10},{10,12},{12,14},{14,16},{16,... | collective-permute-start | bytes 4718600 | tf_op jit(solution)/shard_map/while/body/eval_jaxpr/ppermute | solution.py:12
  552.1 69.3 %collective-permute-start.2 = (f32[128,3072]{1,0:T(8,128)}, f32[128,3072]{1,0:T(8,128)S(1)}, u32[]{:S(2)}, u32[]{:S(2)}) collective-permute-start(f32[128,3072]{1,0:T(8,128)} %get-tuple-element.274), channel_id=1, source_target_pairs={{16,0},{18,2},{20,4},{22,6},{24,8},{26,10},{28,12},{30,14},{0,16},... | collective-permute-start | bytes 4718600 | tf_op jit(solution)/shard_map/ppermute | solution.py:12
  (39 other events, 142.9 us)
Sparse Core Ops, SparseCore 0:
  34.0 20.1 reduce-scatter.2
  95.9 14.7 reduce-scatter.4
  155.4 14.5 reduce-scatter.4
  214.7 14.4 reduce-scatter.4
  274.0 14.4 reduce-scatter.4
  333.3 14.5 reduce-scatter.4
  392.6 14.5 reduce-scatter.4
  452.0 14.5 reduce-scatter.4
  511.3 14.5 reduce-scatter.4
where the time goes:
time: 635 us; the launch traced here: 632 us
  waiting for transfers between devices  286 us (45%)
  blocking collectives  103 us (16%)
  matrix products  102 us (16%)
  local copies, waits for them, and re-layouts  63.8 us (10%)
  other arithmetic  59.3 us (9%)
  between operations  13.3 us (2%)
    ppermute x17, waiting for transfers between devices, from_behind(): return lax.ppermute(block, axis, route)  161 us
    reduce_scatter x9, waiting for transfers between devices, forward(): lax.psum_scatter(jnp.einsum('prf,rft->tp', cross, local_table, preferred_...  124 us
    all_gather x9, blocking collectives, correlate(): spectral = back(lax.all_gather(adjoint, 'lag', axis=1, tiled=True))  58.8 us
    psum x9, blocking collectives, correlate(): lax.psum(jnp.sum(weight[None, :] * lagged * lagged, axis=1) / lag_total,...  44.5 us
    dot_general x9, matrix products, back(): jnp.einsum('pt,rft->prf', piece, local_table, preferred_element_type=jnp....  32.8 us
    dot_general x9, matrix products, visit(): jnp.einsum('ps,pw->sw', pick_second, far, preferred_element_type=jnp.floa...  30.9 us
    another operation x19, other arithmetic  22.6 us
    while x88, local copies, waits for them, and re-layouts  18.4 us
  transfers between devices with their start and end apart: 26, of which 18 were waited for; matrix products, arithmetic and copies ran while one was open for 19% of the time, Pallas kernels for 0%

commit v1 on v0

v1 whole, which is shorter than its diff:
```python
import math

import jax
import jax.numpy as jnp
import ml_dtypes
import numpy as np
from jax import lax
from jax.sharding import PartitionSpec as P

F32 = jnp.float32
BF16 = jnp.bfloat16


def from_behind(block, axis, distance):
    devices = range(lax.axis_size(axis))
    route = [((i - distance) % len(devices), i) for i in devices]
    return lax.ppermute(block, axis, route)


def phase_table(lanes, bins_local):
    freq_total = lanes * bins_local
    lag_total = 2 * freq_total
    turns = np.arange(freq_total)[:, None] * np.arange(lag_total)[None, :] % lag_total
    angle = turns.astype(np.float32) * np.float32(2.0 * np.pi / lag_total)
    factor = np.float32(1.0) / np.sqrt(np.float32(freq_total))
    table = np.stack([np.cos(angle) * factor, -np.sin(angle) * factor], 0)
    table = table.reshape(2, lanes, bins_local, lag_total).transpose(1, 0, 2, 3)
    return table.reshape(lanes * 2 * bins_local, lag_total).astype(ml_dtypes.bfloat16)


def whiten(spectra, band, freq_ids):
    values = spectra.astype(F32)
    meansq = jnp.mean(values * values, axis=(1, 2))
    inside = (freq_ids[None, :] >= band[:, 0:1]) & (freq_ids[None, :] < band[:, 1:2])
    factor = jnp.where(inside, 1.0 / jnp.sqrt(jnp.maximum(meansq, 0.25)), 0.0)
    return (values * factor[:, None, None, :]).astype(BF16)


def in_lane_order(own, received, lane, lanes):
    relative = [own] + received
    backward = [relative[(-m) % lanes] for m in range(lanes)]
    if lanes == 2:
        first = jnp.where(lane == 0, own, received[0])
        second = jnp.where(lane == 0, received[0], own)
        return [first, second]
    stacked = jnp.stack(backward + backward, 0)
    ordered = lax.dynamic_slice_in_dim(stacked, (lanes - lane) % lanes, lanes, 0)
    return [ordered[j] for j in range(lanes)]


def swap_lanes(pieces, lane, lanes):
    stacked = jnp.stack(pieces, 0)
    own = lax.dynamic_index_in_dim(stacked, lane, 0, keepdims=False)
    received = []
    for r in range(1, lanes):
        leaving = lax.dynamic_index_in_dim(stacked, (lane + r) % lanes, 0, keepdims=False)
        received.append(from_behind(leaving, "lag", r))
    return in_lane_order(own, received, lane, lanes)


def on_device(spectra, band, pair_lists, pair_counts):
    stations, comps, parts, bins = spectra.shape
    steps, slots = pair_lists.shape[1:3]
    lanes = lax.axis_size("lag")
    freq_total = bins * lanes
    lag_total = 2 * freq_total
    width = comps * parts * bins
    lane = lax.axis_index("lag")
    freq_ids = lane * bins + jnp.arange(bins, dtype=jnp.int32)
    reach = math.isqrt(steps - 1) + 1
    aheads = list(range(reach))
    behinds = list(range(0, steps, reach))

    slot_ids = jnp.arange(slots, dtype=jnp.int32)
    used = slot_ids[None, :] < pair_counts[0][:, None]
    lists = jnp.where(used[:, :, None], pair_lists[0], stations)
    lists_of = {0: lists}
    for ahead in aheads[1:]:
        lists_of[ahead] = from_behind(lists, "blk", -ahead)
    resident = whiten(spectra, band, freq_ids).reshape(stations, width)
    firsts = {0: resident}
    seconds = {0: resident}
    for ahead in aheads[1:]:
        firsts[ahead] = from_behind(resident, "blk", -ahead)
    order = [0] + behinds[:0:-1]
    for behind in order[1:]:
        seconds[behind] = from_behind(resident, "blk", behind)

    table = jnp.asarray(phase_table(lanes, bins))
    weight = 1.0 + 3.0 * jnp.arange(lag_total, dtype=F32) / lag_total
    station_ids = jnp.arange(stations, dtype=jnp.int32)

    def planes(rows):
        return [rows[:, i * bins : (i + 1) * bins].astype(F32) for i in range(comps * parts)]

    total_first = {ahead: [] for ahead in aheads}
    returned = []
    for behind in order:
        active = [ahead for ahead in aheads if ahead + behind < steps]
        chosen = jnp.concatenate([lists_of[a][a + behind] for a in active], 0)
        pick_first = (chosen[:, 0:1] == station_ids[None, :]).astype(BF16)
        pick_second = (chosen[:, 1:2] == station_ids[None, :]).astype(BF16)
        rows_a = jnp.concatenate(
            [
                jnp.dot(pick_first[n * slots : (n + 1) * slots], firsts[a], preferred_element_type=BF16)
                for n, a in enumerate(active)
            ],
            0,
        )
        rows_b = jnp.dot(pick_second, seconds[behind], preferred_element_type=BF16)
        a = planes(rows_a)
        b = planes(rows_b)
        real = sum(a[2 * c] * b[2 * c] + a[2 * c + 1] * b[2 * c + 1] for c in range(comps))
        imag = sum(a[2 * c + 1] * b[2 * c] - a[2 * c] * b[2 * c + 1] for c in range(comps))
        cross = jnp.concatenate([real, imag], 1).astype(BF16)
        share = cross.shape[0] // lanes
        full = jnp.concatenate(
            swap_lanes([cross[j * share : (j + 1) * share] for j in range(lanes)], lane, lanes), 1
        )
        lagged = jnp.dot(full, table, preferred_element_type=F32)
        energy = jnp.sum(weight[None, :] * lagged * lagged, axis=1) / lag_total
        adjoint = (weight[None, :] * lagged / jnp.sqrt(energy + 1e-05)[:, None]).astype(BF16)
        spectral = lax.dot_general(
            adjoint, table, (((1,), (1,)), ((), ())), preferred_element_type=F32
        ).astype(BF16)
        mine = 2 * bins
        spectral = jnp.concatenate(
            swap_lanes([spectral[:, j * mine : (j + 1) * mine] for j in range(lanes)], lane, lanes), 0
        ).astype(F32)
        real = spectral[:, :bins]
        imag = spectral[:, bins:]
        near = []
        far = []
        for c in range(comps):
            near += [real * b[2 * c] - imag * b[2 * c + 1], real * b[2 * c + 1] + imag * b[2 * c]]
            far += [real * a[2 * c] + imag * a[2 * c + 1], real * a[2 * c + 1] - imag * a[2 * c]]
        near = jnp.concatenate(near, 1).astype(BF16)
        far = jnp.concatenate(far, 1).astype(BF16)
        for n, ahead in enumerate(active):
            total_first[ahead].append(
                (pick_first[n * slots : (n + 1) * slots], near[n * slots : (n + 1) * slots])
            )
        if behind == 0:
            total_first[0].append((pick_second, far))
        else:
            back = jnp.einsum("ps,pw->sw", pick_second, far, preferred_element_type=F32)
            returned.append(from_behind(back.astype(BF16), "blk", -behind))

    def scatter(terms):
        picks = jnp.concatenate([pick for pick, _ in terms], 0)
        values = jnp.concatenate([value for _, value in terms], 0)
        return jnp.einsum("ps,pw->sw", picks, values, preferred_element_type=F32)

    for ahead in aheads[:0:-1]:
        returned.append(from_behind(scatter(total_first[ahead]).astype(BF16), "blk", ahead))
    total = scatter(total_first[0])
    for part in returned:
        total = total + part.astype(F32)
    gradient = total / math.sqrt(slots)
    return gradient.reshape(stations, comps, parts, bins)


def solution(mesh):
    in_specs = (
        P("blk", None, None, "lag"),
        P("blk", None),
        P("blk", None, None, None),
        P("blk", None),
    )
    out_specs = P("blk", None, None, "lag")
    return jax.shard_map(
        on_device, mesh=mesh, in_specs=in_specs, out_specs=out_specs, check_vma=False
    )
```

time: 635 us -> 189 us (0.30)
  waiting for transfers between devices: 286 us -> 116 us
  blocking collectives: 103 us -> 0 us
  matrix products: 102 us -> 23.3 us
  local copies, waits for them, and re-layouts: 63.8 us -> 5.76 us
  other arithmetic: 59.3 us -> 17.9 us
  starting transfers between devices: 3.38 us -> 21.1 us
  between operations: 13.3 us -> 1.15 us
    reduce_scatter x9 -> x0, waiting for transfers between devices: 124 us -> none  [forward(): lax.psum_scatter(jnp.einsum('prf,rft->tp', cross, local_table, preferred_...]
    dot_general x54 -> x26, matrix products: 102 us -> 23.3 us  [the longest x3 8.9 us: on_device(): lax.dot_general(adjoint, table, (((1,), (1,)), ((), ())), preferred_eleme...]
    all_gather x9 -> x0, blocking collectives: 58.8 us -> none  [correlate(): spectral = back(lax.all_gather(adjoint, 'lag', axis=1, tiled=True))]
    ppermute x17 -> x16, waiting for transfers between devices: 161 us -> 116 us  [from_behind(): return lax.ppermute(block, axis, route)]
    psum x9 -> x0, blocking collectives: 44.5 us -> none  [correlate(): lax.psum(jnp.sum(weight[None, :] * lagged * lagged, axis=1) / lag_total,...]
    another operation x29 -> x9, other arithmetic: 28 us -> 2.9 us
    while x88 -> x0, local copies, waits for them, and re-layouts: 18.4 us -> none
    ppermute x17 -> x16, starting transfers between devices: 3.13 us -> 21.1 us  [from_behind(): return lax.ppermute(block, axis, route)]
  transfers between devices with their start and end apart: 26 -> 16, of which waited for: 18 -> 11; matrix products, arithmetic and copies ran while one was open for 19% -> 15% of each run, Pallas kernels for 0% -> 0%
where the time goes in v1:
time: 189 us; the launch traced here: 185 us
  waiting for transfers between devices  116 us (61%)
  matrix products  23.3 us (12%)
  starting transfers between devices  21.1 us (11%)
  other arithmetic  17.9 us (9%)
  local copies, waits for them, and re-layouts  5.76 us (3%)
    ppermute x16, waiting for transfers between devices, from_behind(): return lax.ppermute(block, axis, route)  116 us
    ppermute x16, starting transfers between devices, from_behind(): return lax.ppermute(block, axis, route)  21.1 us
    dot_general x3, matrix products, on_device(): lax.dot_general(adjoint, table, (((1,), (1,)), ((), ())), preferred_eleme...  8.9 us
    dot_general x6, matrix products, on_device(): lagged = jnp.dot(full, table, preferred_element_type=F32)  5.95 us
    unnamed x25, other arithmetic  5.93 us
  transfers between devices with their start and end apart: 16, of which 11 were waited for; matrix products, arithmetic and copies ran while one was open for 15% of the time, Pallas kernels for 0%

profile of v1, /device:TPU:0, one launch (start us, length us, event | category | flops | bytes accessed | tf_op | source)
XLA Modules:
  0.0 185.3 jit_solution(14307550346198137213)
XLA Ops:
  1.5 5.4 %collective-permute-start = (s32[9,96,2]{1,2,0:T(2,128)S(1)}, s32[9,96,2]{1,2,0:T(2,128)S(1)}, u32[]{:S(2)}, u32[]{:S(2)}) collective-permute-start(s32[9,96,2]{1,2,0:T(2,128)S(1)} %bitcast_select_fusion), channel_id=1, source_target_pairs={{2,0},{4,2},{6,4},{8,6},{10,8},{12,10},{14,12},{16,14},{18,16},{20... | collective-permute-start | bytes 20744 | tf_op jit(solution)/shard_map/ppermute | solution.py:17
  8.3 2.4 %fusion.18 = f32[128,512]{1,0:T(8,128)S(1)} fusion(bf16[128,3,2,512]{3,2,1,0:T(2,128)(2,1)} %param.5), kind=kLoop, calls=%fused_computation.39 | loop fusion | flops 1114112 | bytes 1048576 | tf_op jit(solution)/shard_map/reduce_sum | solution.py:33
  12.3 1.3 collective-permute-start.3
  13.8 1.0 collective-permute-start.9
  17.0 16.1 %collective-permute-done.3 = bf16[128,3072]{1,0:T(8,128)(2,1)S(1)} collective-permute-done((bf16[128,3072]{1,0:T(8,128)(2,1)S(1)}, bf16[128,3072]{1,0:T(8,128)(2,1)S(1)}, u32[]{:S(2)}, u32[]{:S(2)}) %collective-permute-start.3) | collective-permute-done | bytes 786464 | tf_op jit(solution)/shard_map/ppermute | solution.py:17
  33.4 15.2 %collective-permute-done.2 = bf16[128,3072]{1,0:T(8,128)(2,1)S(1)} collective-permute-done((bf16[128,3072]{1,0:T(8,128)(2,1)S(1)}, bf16[128,3072]{1,0:T(8,128)(2,1)S(1)}, u32[]{:S(2)}, u32[]{:S(2)}) %collective-permute-start.2) | collective-permute-done | bytes 786464 | tf_op jit(solution)/shard_map/ppermute | solution.py:17
  50.7 18.4 %collective-permute-done.6 = bf16[128,3072]{1,0:T(8,128)(2,1)S(1)} collective-permute-done((bf16[128,3072]{1,0:T(8,128)(2,1)S(1)}, bf16[128,3072]{1,0:T(8,128)(2,1)S(1)}, u32[]{:S(2)}, u32[]{:S(2)}) %collective-permute-start.6) | collective-permute-done | bytes 786464 | tf_op jit(solution)/shard_map/ppermute | solution.py:17
  73.3 1.6 collective-permute-start.4
  75.8 1.6 collective-permute-start.10
  77.4 5.9 %collective-permute-done.4 = bf16[144,1024]{1,0:T(8,128)(2,1)S(1)} collective-permute-done((bf16[144,1024]{1,0:T(8,128)(2,1)S(1)}, bf16[144,1024]{1,0:T(8,128)(2,1)S(1)}, u32[]{:S(2)}, u32[]{:S(2)}) %collective-permute-start.4) | collective-permute-done | bytes 294944 | tf_op jit(solution)/shard_map/ppermute | solution.py:17
  83.3 0.9 fusion.206
  84.2 5.4 %collective-permute-done.7 = bf16[144,1024]{1,0:T(8,128)(2,1)S(1)} collective-permute-done((bf16[144,1024]{1,0:T(8,128)(2,1)S(1)}, bf16[144,1024]{1,0:T(8,128)(2,1)S(1)}, u32[]{:S(2)}, u32[]{:S(2)}) %collective-permute-start.7) | collective-permute-done | bytes 294944 | tf_op jit(solution)/shard_map/ppermute | solution.py:17
  89.6 0.9 fusion.207
  90.5 4.0 %collective-permute-done.10 = bf16[144,1024]{1,0:T(8,128)(2,1)S(1)} collective-permute-done((bf16[144,1024]{1,0:T(8,128)(2,1)S(1)}, bf16[144,1024]{1,0:T(8,128)(2,1)S(1)}, u32[]{:S(2)}, u32[]{:S(2)}) %collective-permute-start.10) | collective-permute-done | bytes 294944 | tf_op jit(solution)/shard_map/ppermute | solution.py:17
  94.5 0.9 fusion.208
  95.4 0.9 convolution_add_fusion.1
  96.4 1.1 convolution_add_fusion
  97.5 1.2 fusion.20
  98.7 1.3 slice-done.1
  100.1 3.0 %convolution_convert_fusion.6 = bf16[144,2048]{1,0:T(8,128)(2,1)S(1)} fusion(bf16[2048,2048]{1,0:T(8,128)(2,1)S(1)} %bitcast.130, f32[144,2048]{1,0:T(8,128)S(1)} %get-tuple-element.79, f32[144]{0:T(256)S(1)} %add_sqrt_fusion.2, f32[2048]{0:T(1024)S(1)} %multiply_add_fusion), kind=kOutput, calls=%fused_computation.17 | convolution fusion | flops 1209139200 | bytes 10166848 | tf_op jit(solution)/shard_map/dot_general | solution.py:123
  103.2 1.5 collective-permute-start.5
  104.7 3.0 %convolution_convert_fusion.5 = bf16[144,2048]{1,0:T(8,128)(2,1)S(1)} fusion(bf16[2048,2048]{1,0:T(8,128)(2,1)S(1)} %bitcast.130, f32[144,2048]{1,0:T(8,128)S(1)} %convolution_add_fusion.1, f32[144]{0:T(256)S(1)} %add_sqrt_fusion.1, f32[2048]{0:T(1024)S(1)} %multiply_add_fusion), kind=kOutput, calls=%fused_computation.16 | convolution fusion | flops 1209139200 | bytes 10166848 | tf_op jit(solution)/shard_map/dot_general | solution.py:123
  108.5 3.0 %convolution_convert_fusion.4 = bf16[144,2048]{1,0:T(8,128)(2,1)S(1)} fusion(bf16[2048,2048]{1,0:T(8,128)(2,1)S(1)} %bitcast.130, f32[144,2048]{1,0:T(8,128)S(1)} %convolution_add_fusion, f32[144]{0:T(256)S(1)} %add_sqrt_fusion, f32[2048]{0:T(1024)S(1)} %multiply_add_fusion), kind=kOutput, calls=%fused_computation.15 | convolution fusion | flops 1209139200 | bytes 10166848 | tf_op jit(solution)/shard_map/dot_general | solution.py:123
  111.7 1.5 collective-permute-start.11
  116.1 2.9 %collective-permute-done.8 = bf16[144,1024]{1,0:T(8,128)(2,1)S(1)} collective-permute-done((bf16[144,1024]{1,0:T(8,128)(2,1)S(1)}, bf16[144,1024]{1,0:T(8,128)(2,1)S(1)}, u32[]{:S(2)}, u32[]{:S(2)}) %collective-permute-start.8) | collective-permute-done | bytes 294944 | tf_op jit(solution)/shard_map/ppermute | solution.py:17
  122.1 1.3 collective-permute-done.11
  129.2 5.0 %collective-permute-start.13 = (bf16[128,3072]{1,0:T(8,128)(2,1)S(1)}, bf16[128,3072]{1,0:T(8,128)(2,1)S(1)}, u32[]{:S(2)}, u32[]{:S(2)}) collective-permute-start(bf16[128,3072]{1,0:T(8,128)(2,1)S(1)} %convolution_convert_fusion.2), channel_id=1, source_target_pairs={{6,0},{8,2},{10,4},{12,6},{14,8},{16,10},{18,12},{20,14},{22,16},{... | collective-permute-start | bytes 2359304 | tf_op jit(solution)/shard_map/ppermute | solution.py:17
  134.4 36.0 %collective-permute-done.14 = bf16[128,3072]{1,0:T(8,128)(2,1)S(1)} collective-permute-done((bf16[128,3072]{1,0:T(8,128)(2,1)S(1)}, bf16[128,3072]{1,0:T(8,128)(2,1)S(1)}, u32[]{:S(2)}, u32[]{:S(2)}) %collective-permute-start.14) | collective-permute-done | bytes 786464 | tf_op jit(solution)/shard_map/ppermute | solution.py:17
  170.3 2.6 %collective-permute-done.12 = bf16[128,3072]{1,0:T(8,128)(2,1)S(1)} collective-permute-done((bf16[128,3072]{1,0:T(8,128)(2,1)S(1)}, bf16[128,3072]{1,0:T(8,128)(2,1)S(1)}, u32[]{:S(2)}, u32[]{:S(2)}) %collective-permute-start.12) | collective-permute-done | bytes 786464 | tf_op jit(solution)/shard_map/ppermute | solution.py:17
  172.9 8.3 %collective-permute-done.13 = bf16[128,3072]{1,0:T(8,128)(2,1)S(1)} collective-permute-done((bf16[128,3072]{1,0:T(8,128)(2,1)S(1)}, bf16[128,3072]{1,0:T(8,128)(2,1)S(1)}, u32[]{:S(2)}, u32[]{:S(2)}) %collective-permute-start.13) | collective-permute-done | bytes 786464 | tf_op jit(solution)/shard_map/ppermute | solution.py:17
  181.2 1.1 add_multiply_fusion
  182.3 2.5 %reshape.110 = f32[128,3,2,512]{3,2,1,0:T(2,128)} reshape(f32[128,3072]{1,0:T(8,128)S(1)} %add_multiply_fusion) | data formatting | bytes 3145728 | tf_op jit(solution)/shard_map/reshape | solution.py:160
  (125 shorter events, 26.9 us)
Async XLA Ops:
  0.0 10.9 %copy-start.2 = (bf16[128,3,2,512]{3,2,1,0:T(2,128)(2,1)S(1)}, bf16[128,3,2,512]{3,2,1,0:T(2,128)(2,1)}, u32[]{:S(2)}) copy-start(bf16[128,3,2,512]{3,2,1,0:T(2,128)(2,1)} %param.5) | copy-start | bytes 2359300
  1.5 12.3 %collective-permute-start = (s32[9,96,2]{1,2,0:T(2,128)S(1)}, s32[9,96,2]{1,2,0:T(2,128)S(1)}, u32[]{:S(2)}, u32[]{:S(2)}) collective-permute-start(s32[9,96,2]{1,2,0:T(2,128)S(1)} %bitcast_select_fusion), channel_id=1, source_target_pairs={{2,0},{4,2},{6,4},{8,6},{10,8},{12,10},{14,12},{16,14},{18,16},{20... | collective-permute-start | bytes 20744 | tf_op jit(solution)/shard_map/ppermute | solution.py:17
  7.0 7.8 %collective-permute-start.1 = (s32[9,96,2]{1,2,0:T(2,128)S(1)}, s32[9,96,2]{1,2,0:T(2,128)S(1)}, u32[]{:S(2)}, u32[]{:S(2)}) collective-permute-start(s32[9,96,2]{1,2,0:T(2,128)S(1)} %bitcast_select_fusion), channel_id=1, source_target_pairs={{4,0},{6,2},{8,4},{10,6},{12,8},{14,10},{16,12},{18,14},{20,16},{2... | collective-permute-start | bytes 20744 | tf_op jit(solution)/shard_map/ppermute | solution.py:17
  12.3 20.8 %collective-permute-start.3 = (bf16[128,3072]{1,0:T(8,128)(2,1)S(1)}, bf16[128,3072]{1,0:T(8,128)(2,1)S(1)}, u32[]{:S(2)}, u32[]{:S(2)}) collective-permute-start(bf16[128,3072]{1,0:T(8,128)(2,1)S(1)} %reshape.109), channel_id=1, source_target_pairs={{4,0},{6,2},{8,4},{10,6},{12,8},{14,10},{16,12},{18,14},{20,16},{2... | collective-permute-start | bytes 2359304 | tf_op jit(solution)/shard_map/ppermute | solution.py:17
  13.7 34.9 %collective-permute-start.2 = (bf16[128,3072]{1,0:T(8,128)(2,1)S(1)}, bf16[128,3072]{1,0:T(8,128)(2,1)S(1)}, u32[]{:S(2)}, u32[]{:S(2)}) collective-permute-start(bf16[128,3072]{1,0:T(8,128)(2,1)S(1)} %reshape.109), channel_id=1, source_target_pairs={{2,0},{4,2},{6,4},{8,6},{10,8},{12,10},{14,12},{16,14},{18,16},{20... | collective-permute-start | bytes 2359304 | tf_op jit(solution)/shard_map/ppermute | solution.py:17
  13.8 55.3 %collective-permute-start.6 = (bf16[128,3072]{1,0:T(8,128)(2,1)S(1)}, bf16[128,3072]{1,0:T(8,128)(2,1)S(1)}, u32[]{:S(2)}, u32[]{:S(2)}) collective-permute-start(bf16[128,3072]{1,0:T(8,128)(2,1)S(1)} %reshape.109), channel_id=1, source_target_pairs={{20,0},{22,2},{24,4},{26,6},{28,8},{30,10},{0,12},{2,14},{4,16},{6... | collective-permute-start | bytes 2359304 | tf_op jit(solution)/shard_map/ppermute | solution.py:17
  13.8 57.7 %collective-permute-start.9 = (bf16[128,3072]{1,0:T(8,128)(2,1)S(1)}, bf16[128,3072]{1,0:T(8,128)(2,1)S(1)}, u32[]{:S(2)}, u32[]{:S(2)}) collective-permute-start(bf16[128,3072]{1,0:T(8,128)(2,1)S(1)} %reshape.109), channel_id=1, source_target_pairs={{26,0},{28,2},{30,4},{0,6},{2,8},{4,10},{6,12},{8,14},{10,16},{12,... | collective-permute-start | bytes 2359304 | tf_op jit(solution)/shard_map/ppermute | solution.py:17
  73.2 10.1 %copy-start.1 = (bf16[1024,2048]{1,0:T(8,128)(2,1)S(1)}, bf16[1024,2048]{1,0:T(8,128)(2,1)}, u32[]{:S(2)}) copy-start(bf16[1024,2048]{1,0:T(8,128)(2,1)} %constant.90) | copy-start | bytes 12582916
  73.3 10.0 %collective-permute-start.4 = (bf16[144,1024]{1,0:T(8,128)(2,1)S(1)}, bf16[144,1024]{1,0:T(8,128)(2,1)S(1)}, u32[]{:S(2)}, u32[]{:S(2)}) collective-permute-start(bf16[144,1024]{1,0:T(8,128)(2,1)S(1)} %fusion.200), channel_id=1, source_target_pairs={{1,0},{0,1},{3,2},{2,3},{5,4},{4,5},{7,6},{6,7},{9,8},{8,9},{11,10... | collective-permute-start | bytes 884744 | tf_op jit(solution)/shard_map/ppermute | solution.py:17
  75.0 14.6 %collective-permute-start.7 = (bf16[144,1024]{1,0:T(8,128)(2,1)S(1)}, bf16[144,1024]{1,0:T(8,128)(2,1)S(1)}, u32[]{:S(2)}, u32[]{:S(2)}) collective-permute-start(bf16[144,1024]{1,0:T(8,128)(2,1)S(1)} %fusion.192), channel_id=1, source_target_pairs={{1,0},{0,1},{3,2},{2,3},{5,4},{4,5},{7,6},{6,7},{9,8},{8,9},{11,10... | collective-permute-start | bytes 884744 | tf_op jit(solution)/shard_map/ppermute | solution.py:17
  75.8 18.7 %collective-permute-start.10 = (bf16[144,1024]{1,0:T(8,128)(2,1)S(1)}, bf16[144,1024]{1,0:T(8,128)(2,1)S(1)}, u32[]{:S(2)}, u32[]{:S(2)}) collective-permute-start(bf16[144,1024]{1,0:T(8,128)(2,1)S(1)} %fusion.184), channel_id=1, source_target_pairs={{1,0},{0,1},{3,2},{2,3},{5,4},{4,5},{7,6},{6,7},{9,8},{8,9},{11,10... | collective-permute-start | bytes 884744 | tf_op jit(solution)/shard_map/ppermute | solution.py:17
  90.5 4.9 %copy-start = (bf16[1024,2048]{1,0:T(8,128)(2,1)S(1)}, bf16[1024,2048]{1,0:T(8,128)(2,1)}, u32[]{:S(2)}) copy-start(bf16[1024,2048]{1,0:T(8,128)(2,1)} %constant.89) | copy-start | bytes 12582916
  96.3 2.4 %slice-start = ((s8[8388608]{0:T(1024)(128)(4,1)}), s8[4194304]{0:T(1024)(128)(4,1)S(1)}, s32[]{:S(2)}) async-start(s8[8388608]{0:T(1024)(128)(4,1)} %bitcast.129), calls=%async_computation | async-start | bytes 8388608
  97.5 2.6 %slice-start.1 = ((s8[8388608]{0:T(1024)(128)(4,1)}), s8[4194304]{0:T(1024)(128)(4,1)S(1)}, s32[]{:S(2)}) async-start(s8[8388608]{0:T(1024)(128)(4,1)} %bitcast.129), calls=%async_computation.1 | async-start | bytes 8388608
  103.2 10.0 %collective-permute-start.5 = (bf16[144,1024]{1,0:T(8,128)(2,1)S(1)}, bf16[144,1024]{1,0:T(8,128)(2,1)S(1)}, u32[]{:S(2)}, u32[]{:S(2)}) collective-permute-start(bf16[144,1024]{1,0:T(8,128)(2,1)S(1)} %fusion.196), channel_id=1, source_target_pairs={{1,0},{0,1},{3,2},{2,3},{5,4},{4,5},{7,6},{6,7},{9,8},{8,9},{11,10... | collective-permute-start | bytes 884744 | tf_op jit(solution)/shard_map/ppermute | solution.py:17
  107.9 11.1 %collective-permute-start.8 = (bf16[144,1024]{1,0:T(8,128)(2,1)S(1)}, bf16[144,1024]{1,0:T(8,128)(2,1)S(1)}, u32[]{:S(2)}, u32[]{:S(2)}) collective-permute-start(bf16[144,1024]{1,0:T(8,128)(2,1)S(1)} %fusion.188), channel_id=1, source_target_pairs={{1,0},{0,1},{3,2},{2,3},{5,4},{4,5},{7,6},{6,7},{9,8},{8,9},{11,10... | collective-permute-start | bytes 884744 | tf_op jit(solution)/shard_map/ppermute | solution.py:17
  111.7 11.8 %collective-permute-start.11 = (bf16[144,1024]{1,0:T(8,128)(2,1)S(1)}, bf16[144,1024]{1,0:T(8,128)(2,1)S(1)}, u32[]{:S(2)}, u32[]{:S(2)}) collective-permute-start(bf16[144,1024]{1,0:T(8,128)(2,1)S(1)} %fusion.180), channel_id=1, source_target_pairs={{1,0},{0,1},{3,2},{2,3},{5,4},{4,5},{7,6},{6,7},{9,8},{8,9},{11,10... | collective-permute-start | bytes 884744 | tf_op jit(solution)/shard_map/ppermute | solution.py:17
  127.0 43.3 %collective-permute-start.14 = (bf16[128,3072]{1,0:T(8,128)(2,1)S(1)}, bf16[128,3072]{1,0:T(8,128)(2,1)S(1)}, u32[]{:S(2)}, u32[]{:S(2)}) collective-permute-start(bf16[128,3072]{1,0:T(8,128)(2,1)S(1)} %convolution_convert_fusion.1), channel_id=1, source_target_pairs={{28,0},{30,2},{0,4},{2,6},{4,8},{6,10},{8,12},{10,14},{12,16},{14,... | collective-permute-start | bytes 2359304 | tf_op jit(solution)/shard_map/ppermute | solution.py:17
  127.7 42.6 %collective-permute-start.15 = (bf16[128,3072]{1,0:T(8,128)(2,1)S(1)}, bf16[128,3072]{1,0:T(8,128)(2,1)S(1)}, u32[]{:S(2)}, u32[]{:S(2)}) collective-permute-start(bf16[128,3072]{1,0:T(8,128)(2,1)S(1)} %convolution_convert_fusion), channel_id=1, source_target_pairs={{30,0},{0,2},{2,4},{4,6},{6,8},{8,10},{10,12},{12,14},{14,16},{16,... | collective-permute-start | bytes 2359304 | tf_op jit(solution)/shard_map/ppermute | solution.py:17
  128.5 44.5 %collective-permute-start.12 = (bf16[128,3072]{1,0:T(8,128)(2,1)S(1)}, bf16[128,3072]{1,0:T(8,128)(2,1)S(1)}, u32[]{:S(2)}, u32[]{:S(2)}) collective-permute-start(bf16[128,3072]{1,0:T(8,128)(2,1)S(1)} %convolution_convert_fusion.3), channel_id=1, source_target_pairs={{12,0},{14,2},{16,4},{18,6},{20,8},{22,10},{24,12},{26,14},{28,16}... | collective-permute-start | bytes 2359304 | tf_op jit(solution)/shard_map/ppermute | solution.py:17
  129.2 52.0 %collective-permute-start.13 = (bf16[128,3072]{1,0:T(8,128)(2,1)S(1)}, bf16[128,3072]{1,0:T(8,128)(2,1)S(1)}, u32[]{:S(2)}, u32[]{:S(2)}) collective-permute-start(bf16[128,3072]{1,0:T(8,128)(2,1)S(1)} %convolution_convert_fusion.2), channel_id=1, source_target_pairs={{6,0},{8,2},{10,4},{12,6},{14,8},{16,10},{18,12},{20,14},{22,16},{... | collective-permute-start | bytes 2359304 | tf_op jit(solution)/shard_map/ppermute | solution.py:17

commit v2 on v1

--- a/solution.py
+++ b/solution.py
@@ -80,11 +80,10 @@
     resident = whiten(spectra, band, freq_ids).reshape(stations, width)
     firsts = {0: resident}
     seconds = {0: resident}
+    for behind in behinds[1:]:
+        seconds[behind] = from_behind(seconds[behind - reach], "blk", reach)
     for ahead in aheads[1:]:
-        firsts[ahead] = from_behind(resident, "blk", -ahead)
-    order = [0] + behinds[:0:-1]
-    for behind in order[1:]:
-        seconds[behind] = from_behind(resident, "blk", behind)
+        firsts[ahead] = from_behind(firsts[ahead - 1], "blk", -1)
 
     table = jnp.asarray(phase_table(lanes, bins))
     weight = 1.0 + 3.0 * jnp.arange(lag_total, dtype=F32) / lag_total
@@ -93,26 +92,32 @@
     def planes(rows):
         return [rows[:, i * bins : (i + 1) * bins].astype(F32) for i in range(comps * parts)]
 
-    total_first = {ahead: [] for ahead in aheads}
-    returned = []
-    for behind in order:
-        active = [ahead for ahead in aheads if ahead + behind < steps]
-        chosen = jnp.concatenate([lists_of[a][a + behind] for a in active], 0)
-        pick_first = (chosen[:, 0:1] == station_ids[None, :]).astype(BF16)
-        pick_second = (chosen[:, 1:2] == station_ids[None, :]).astype(BF16)
-        rows_a = jnp.concatenate(
-            [
-                jnp.dot(pick_first[n * slots : (n + 1) * slots], firsts[a], preferred_element_type=BF16)
-                for n, a in enumerate(active)
-            ],
-            0,
-        )
-        rows_b = jnp.dot(pick_second, seconds[behind], preferred_element_type=BF16)
-        a = planes(rows_a)
-        b = planes(rows_b)
-        real = sum(a[2 * c] * b[2 * c] + a[2 * c + 1] * b[2 * c + 1] for c in range(comps))
-        imag = sum(a[2 * c + 1] * b[2 * c] - a[2 * c] * b[2 * c + 1] for c in range(comps))
-        cross = jnp.concatenate([real, imag], 1).astype(BF16)
+    pairs_first = {ahead: [] for ahead in aheads}
+    pairs_second = {behind: [] for behind in behinds}
+    rounds = {}
+    for ahead in aheads:
+        for behind in behinds:
+            if ahead + behind < steps:
+                arrival = max(ahead, behind // reach, 1)
+                rounds.setdefault(arrival, []).append((ahead, behind))
+    after = jnp.int32(0)
+    for arrival in sorted(rounds):
+        active = rounds[arrival]
+        picks = []
+        rows = []
+        crosses = []
+        for ahead, behind in active:
+            chosen = lists_of[ahead][ahead + behind] + after
+            pick_first = (chosen[:, 0:1] == station_ids[None, :]).astype(BF16)
+            pick_second = (chosen[:, 1:2] == station_ids[None, :]).astype(BF16)
+            a = planes(jnp.dot(pick_first, firsts[ahead], preferred_element_type=BF16))
+            b = planes(jnp.dot(pick_second, seconds[behind], preferred_element_type=BF16))
+            real = sum(a[2 * c] * b[2 * c] + a[2 * c + 1] * b[2 * c + 1] for c in range(comps))
+            imag = sum(a[2 * c + 1] * b[2 * c] - a[2 * c] * b[2 * c + 1] for c in range(comps))
+            picks.append((pick_first, pick_second))
+            rows.append((a, b))
+            crosses.append(jnp.concatenate([real, imag], 1).astype(BF16))
+        cross = jnp.concatenate(crosses, 0)
         share = cross.shape[0] // lanes
         full = jnp.concatenate(
             swap_lanes([cross[j * share : (j + 1) * share] for j in range(lanes)], lane, lanes), 1
@@ -123,39 +128,40 @@
         spectral = lax.dot_general(
             adjoint, table, (((1,), (1,)), ((), ())), preferred_element_type=F32
         ).astype(BF16)
+        after = jnp.minimum(jnp.abs(spectral[0, 0]), 0).astype(jnp.int32)
         mine = 2 * bins
         spectral = jnp.concatenate(
             swap_lanes([spectral[:, j * mine : (j + 1) * mine] for j in range(lanes)], lane, lanes), 0
-        ).astype(F32)
-        real = spectral[:, :bins]
-        imag = spectral[:, bins:]
-        near = []
-        far = []
-        for c in range(comps):
-            near += [real * b[2 * c] - imag * b[2 * c + 1], real * b[2 * c + 1] + imag * b[2 * c]]
-            far += [real * a[2 * c] + imag * a[2 * c + 1], real * a[2 * c + 1] - imag * a[2 * c]]
-        near = jnp.concatenate(near, 1).astype(BF16)
-        far = jnp.concatenate(far, 1).astype(BF16)
-        for n, ahead in enumerate(active):
-            total_first[ahead].append(
-                (pick_first[n * slots : (n + 1) * slots], near[n * slots : (n + 1) * slots])
-            )
-        if behind == 0:
-            total_first[0].append((pick_second, far))
-        else:
-            back = jnp.einsum("ps,pw->sw", pick_second, far, preferred_element_type=F32)
-            returned.append(from_behind(back.astype(BF16), "blk", -behind))
+        )
+        for n, (ahead, behind) in enumerate(active):
+            a, b = rows[n]
+            listed = spectral[n * slots : (n + 1) * slots].astype(F32)
+            real = listed[:, :bins]
+            imag = listed[:, bins:]
+            near = []
+            far = []
+            for c in range(comps):
+                near += [real * b[2 * c] - imag * b[2 * c + 1], real * b[2 * c + 1] + imag * b[2 * c]]
+                far += [real * a[2 * c] + imag * a[2 * c + 1], real * a[2 * c + 1] - imag * a[2 * c]]
+            near = jnp.concatenate(near, 1).astype(BF16)
+            far = jnp.concatenate(far, 1).astype(BF16)
+            pairs_first[ahead].append((picks[n][0], near))
+            pairs_second[behind].append((picks[n][1], far))
 
     def scatter(terms):
         picks = jnp.concatenate([pick for pick, _ in terms], 0)
         values = jnp.concatenate([value for _, value in terms], 0)
         return jnp.einsum("ps,pw->sw", picks, values, preferred_element_type=F32)
 
+    from_ahead = jnp.zeros((), F32)
+    from_back = jnp.zeros((), F32)
+    for behind in behinds[:0:-1]:
+        part = scatter(pairs_second[behind]) + from_back
+        from_back = from_behind(part.astype(BF16), "blk", -reach).astype(F32)
     for ahead in aheads[:0:-1]:
-        returned.append(from_behind(scatter(total_first[ahead]).astype(BF16), "blk", ahead))
-    total = scatter(total_first[0])
-    for part in returned:
-        total = total + part.astype(F32)
+        part = scatter(pairs_first[ahead]) + from_ahead
+        from_ahead = from_behind(part.astype(BF16), "blk", 1).astype(F32)
+    total = scatter(pairs_first[0] + pairs_second[0]) + from_back + from_ahead
     gradient = total / math.sqrt(slots)
     return gradient.reshape(stations, comps, parts, bins)
 

time: 189 us -> 165 us (0.87); the launches traced: 185 us -> 164 us
  waiting for transfers between devices: 116 us -> 68.3 us
  matrix products: 23.3 us -> 40.3 us
  other arithmetic: 17.9 us -> 27.3 us
  starting transfers between devices: 21.1 us -> 17.1 us
  local copies, waits for them, and re-layouts: 5.76 us -> 9.04 us
    ppermute x16 -> x14, waiting for transfers between devices: 116 us -> 68.3 us  [from_behind(): return lax.ppermute(block, axis, route)]
    dot_general x14 -> x18, matrix products: 6.14 us -> 21.8 us  [the longest x9 11.3 us: on_device(): a = planes(jnp.dot(pick_first, firsts[ahead], preferred_element_type=BF16))]
    ppermute x16 -> x14, starting transfers between devices: 21.1 us -> 17.1 us  [from_behind(): return lax.ppermute(block, axis, route)]
    eq x0 -> x12, other arithmetic: none -> 3.34 us  [the longest x6 1.67 us: on_device(): pick_first = (chosen[:, 0:1] == station_ids[None, :]).astype(BF16)]
    unnamed x25 -> x91, other arithmetic: 5.93 us -> 8.95 us
    dot_general x3 -> x5, matrix products: 2.33 us -> 4.4 us  [scatter(): return jnp.einsum('ps,pw->sw', picks, values, preferred_element_type=F32)]
    add x0 -> x3, other arithmetic: none -> 2.03 us  [on_device(): chosen = lists_of[ahead][ahead + behind] + after]
    dot_general x6 -> x4, matrix products: 5.95 us -> 5.38 us  [on_device(): lagged = jnp.dot(full, table, preferred_element_type=F32)]
  transfers between devices with their start and end apart: 16 -> 14, of which waited for: 11 -> 6; matrix products, arithmetic and copies ran while one was open for 15% -> 34% of each run, Pallas kernels for 0% -> 0%
where the time goes in v2:
time: 165 us; the launch traced here: 164 us
  waiting for transfers between devices  68.3 us (41%)
  matrix products  40.3 us (24%)
  other arithmetic  27.3 us (17%)
  starting transfers between devices  17.1 us (10%)
  local copies, waits for them, and re-layouts  9.04 us (5%)
  between operations  2.15 us (1%)
    ppermute x14, waiting for transfers between devices, from_behind(): return lax.ppermute(block, axis, route)  68.3 us
    ppermute x14, starting transfers between devices, from_behind(): return lax.ppermute(block, axis, route)  17.1 us
    dot_general x9, matrix products, on_device(): a = planes(jnp.dot(pick_first, firsts[ahead], preferred_element_type=BF16))  11.3 us
    dot_general x9, matrix products, on_device(): jnp.dot(pick_second, seconds[behind], preferred_element_type=BF16)  10.5 us
    unnamed x91, other arithmetic  8.95 us
    dot_general x2, matrix products, on_device(): lax.dot_general(adjoint, table, (((1,), (1,)), ((), ())), preferred_eleme...  8.72 us
    dot_general x4, matrix products, on_device(): lagged = jnp.dot(full, table, preferred_element_type=F32)  5.38 us
    dot_general x5, matrix products, scatter(): return jnp.einsum('ps,pw->sw', picks, values, preferred_element_type=F32)  4.4 us
  transfers between devices with their start and end apart: 14, of which 6 were waited for; matrix products, arithmetic and copies ran while one was open for 34% of the time, Pallas kernels for 0%

profile of v2, /device:TPU:0, one launch (start us, length us, event | category | flops | bytes accessed | tf_op | source)
XLA Modules:
  0.0 164.2 jit_solution(9352682712703986694)
XLA Ops:
  0.7 1.3 bitcast_select_fusion
  2.0 5.4 %collective-permute-start.1 = (s32[9,96,2]{1,2,0:T(2,128)}, s32[9,96,2]{1,2,0:T(2,128)S(1)}, u32[]{:S(2)}, u32[]{:S(2)}) collective-permute-start(s32[9,96,2]{1,2,0:T(2,128)} %bitcast_select_fusion), channel_id=1, source_target_pairs={{2,0},{4,2},{6,4},{8,6},{10,8},{12,10},{14,12},{16,14},{18,16},{20... | collective-permute-start | bytes 20744 | tf_op jit(solution)/shard_map/ppermute | solution.py:17
  8.8 2.4 %fusion.24 = f32[128,512]{1,0:T(8,128)S(1)} fusion(bf16[128,3,2,512]{3,2,1,0:T(2,128)(2,1)} %param.5), kind=kLoop, calls=%fused_computation.36 | loop fusion | flops 1114112 | bytes 1048576 | tf_op jit(solution)/shard_map/reduce_sum | solution.py:33
  11.3 1.9 %fusion.25 = bf16[128,3,2,512]{3,2,1,0:T(2,128)(2,1)S(1)} fusion(bf16[128,3,2,512]{3,2,1,0:T(2,128)(2,1)} %param.5, f32[128,512]{1,0:T(8,128)S(1)} %rsqrt_select_fusion), kind=kLoop, calls=%fused_computation.37 | loop fusion | flops 1179648 | bytes 1835008 | tf_op jit(solution)/shard_map/convert_element_type | solution.py:36
  20.5 11.2 %collective-permute-done.2 = bf16[128,3072]{1,0:T(8,128)(2,1)} collective-permute-done((bf16[128,3072]{1,0:T(8,128)(2,1)S(1)}, bf16[128,3072]{1,0:T(8,128)(2,1)}, u32[]{:S(2)}, u32[]{:S(2)}) %collective-permute-start.2) | collective-permute-done | bytes 786464 | tf_op jit(solution)/shard_map/ppermute | solution.py:17
  31.7 1.5 fusion.454
  33.6 1.9 %fusion.455 = bf16[96,3072]{1,0:T(8,128)(2,1)S(1)} fusion(bf16[128,3072]{1,0:T(8,128)(2,1)} %collective-permute-done.2, s32[96]{0:T(128)S(1)} %get-tuple-element.63), kind=kOutput, calls=%fused_computation.970 | convolution fusion | flops 75509760 | bytes 1376640 | tf_op jit(solution)/shard_map/dot_general | solution.py:113
  35.5 1.7 %fusion.456 = bf16[96,3072]{1,0:T(8,128)(2,1)S(1)} fusion(bf16[128,3072]{1,0:T(8,128)(2,1)} %collective-permute-done, s32[96]{0:T(128)S(1)} %get-tuple-element.64), kind=kOutput, calls=%fused_computation.971 | convolution fusion | flops 75509760 | bytes 1376640 | tf_op jit(solution)/shard_map/dot_general | solution.py:114
  37.5 1.6 %fusion.453 = bf16[96,3072]{1,0:T(8,128)(2,1)S(1)} fusion(bf16[128,3072]{1,0:T(8,128)(2,1)} %collective-permute-done, s32[96]{0:T(128)S(1)} %get-tuple-element.68), kind=kOutput, calls=%fused_computation.968 | convolution fusion | flops 75509760 | bytes 1376640 | tf_op jit(solution)/shard_map/dot_general | solution.py:114
  40.5 1.6 collective-permute-start.3
  43.4 4.4 %collective-permute-start.7 = (bf16[128,3072]{1,0:T(8,128)(2,1)}, bf16[128,3072]{1,0:T(8,128)(2,1)}, u32[]{:S(2)}, u32[]{:S(2)}) collective-permute-start(bf16[128,3072]{1,0:T(8,128)(2,1)} %collective-permute-done.2), channel_id=1, source_target_pairs={{2,0},{4,2},{6,4},{8,6},{10,8},{12,10},{14,12},{16,14},{18,16},{20... | collective-permute-start | bytes 2359304 | tf_op jit(solution)/shard_map/ppermute | solution.py:17
  47.8 4.6 %collective-permute-done.3 = bf16[192,1024]{1,0:T(8,128)(2,1)S(1)} collective-permute-done((bf16[192,1024]{1,0:T(8,128)(2,1)S(1)}, bf16[192,1024]{1,0:T(8,128)(2,1)S(1)}, u32[]{:S(2)}, u32[]{:S(2)}) %collective-permute-start.3) | collective-permute-done | bytes 393248 | tf_op jit(solution)/shard_map/ppermute | solution.py:17
  53.5 1.3 fusion.26
  54.9 2.9 %convolution_convert_fusion.3 = bf16[192,2048]{1,0:T(8,128)(2,1)S(1)} fusion(bf16[2048,2048]{1,0:T(8,128)(2,1)S(1)} %bitcast.147, f32[192,2048]{1,0:T(8,128)S(1)} %get-tuple-element.72, f32[192]{0:T(256)S(1)} %add_sqrt_fusion.1, f32[2048]{0:T(1024)S(1)} %multiply_add_fusion), kind=kOutput, calls=%fused_computation.7 | convolution fusion | flops 1612185600 | bytes 10756864 | tf_op jit(solution)/shard_map/dot_general | solution.py:128
  64.4 2.5 %collective-permute-start.5 = (bf16[192,1024]{1,0:T(8,128)(2,1)S(1)}, bf16[192,1024]{1,0:T(8,128)(2,1)S(1)}, u32[]{:S(2)}, u32[]{:S(2)}) collective-permute-start(bf16[192,1024]{1,0:T(8,128)(2,1)S(1)} %fusion.50), channel_id=1, source_target_pairs={{1,0},{0,1},{3,2},{2,3},{5,4},{4,5},{7,6},{6,7},{9,8},{8,9},{11,10... | collective-permute-start | bytes 1179656 | tf_op jit(solution)/shard_map/ppermute | solution.py:17
  67.4 1.5 fusion.462
  68.9 1.5 fusion.458
  70.4 1.5 fusion.461
  72.2 1.5 fusion.459
  74.1 1.5 fusion.464
  75.6 1.5 fusion.463
  77.4 1.5 fusion.457
  79.2 1.5 fusion.460
  89.0 6.0 %collective-permute-done.8 = bf16[240,1024]{1,0:T(8,128)(2,1)S(1)} collective-permute-done((bf16[240,1024]{1,0:T(8,128)(2,1)S(1)}, bf16[240,1024]{1,0:T(8,128)(2,1)S(1)}, u32[]{:S(2)}, u32[]{:S(2)}) %collective-permute-start.8) | collective-permute-done | bytes 491552 | tf_op jit(solution)/shard_map/ppermute | solution.py:17
  95.0 1.5 fusion.44
  96.5 1.5 fusion
  98.0 5.8 %convolution_convert_fusion.2 = bf16[240,2048]{1,0:T(8,128)(2,1)S(1)} fusion(bf16[2048,2048]{1,0:T(8,128)(2,1)} %constant.80.clone, f32[240,2048]{1,0:T(8,128)S(1)} %get-tuple-element.74, f32[240]{0:T(256)S(1)} %add_sqrt_fusion, f32[2048]{0:T(1024)S(1)} %multiply_add_fusion), kind=kOutput, calls=%fused_computation.6 | convolution fusion | flops 2015232000 | bytes 11346880 | tf_op jit(solution)/shard_map/dot_general | solution.py:128
  104.6 11.9 %collective-permute-done.9 = bf16[240,1024]{1,0:T(8,128)(2,1)S(1)} collective-permute-done((bf16[240,1024]{1,0:T(8,128)(2,1)S(1)}, bf16[240,1024]{1,0:T(8,128)(2,1)S(1)}, u32[]{:S(2)}, u32[]{:S(2)}) %collective-permute-start.9) | collective-permute-done | bytes 491552 | tf_op jit(solution)/shard_map/ppermute | solution.py:17
  123.0 16.8 %collective-permute-done.10 = bf16[128,3072]{1,0:T(8,128)(2,1)S(1)} collective-permute-done((bf16[128,3072]{1,0:T(8,128)(2,1)S(1)}, bf16[128,3072]{1,0:T(8,128)(2,1)S(1)}, u32[]{:S(2)}, u32[]{:S(2)}) %collective-permute-start.10) | collective-permute-done | bytes 786464 | tf_op jit(solution)/shard_map/ppermute | solution.py:17
  139.8 1.7 %add_convert_fusion.1 = bf16[128,3072]{1,0:T(8,128)(2,1)S(1)} fusion(bf16[128,3072]{1,0:T(8,128)(2,1)S(1)} %collective-permute-done.10, bf16[96,3072]{1,0:T(8,128)(2,1)S(1)} %get-tuple-element.24, bf16[96,3072]{1,0:T(8,128)(2,1)S(1)} %copy-done.16, bf16[96,3072]{1,0:T(8,128)(2,1)} %get-tuple-element.18, pred[96,128]{1,0:T(32,128)(4,1)S(1)} %iota_compare_fusion.2, ...), kind=kOutput, calls=%fused_computation.42 | convolution fusion | flops 233054208 | bytes 3379200 | tf_op jit(solution)/shard_map/ps,pw->sw/dot_general | solution.py:154
  143.6 17.8 %collective-permute-done.11 = bf16[128,3072]{1,0:T(8,128)(2,1)S(1)} collective-permute-done((bf16[128,3072]{1,0:T(8,128)(2,1)S(1)}, bf16[128,3072]{1,0:T(8,128)(2,1)S(1)}, u32[]{:S(2)}, u32[]{:S(2)}) %collective-permute-start.11) | collective-permute-done | bytes 786464 | tf_op jit(solution)/shard_map/ppermute | solution.py:17
  161.7 2.5 %reshape.120 = f32[128,3,2,512]{3,2,1,0:T(2,128)} reshape(f32[128,3072]{1,0:T(8,128)S(1)} %add_multiply_fusion) | data formatting | bytes 3145728 | tf_op jit(solution)/shard_map/reshape | solution.py:166
  (253 shorter events, 38.2 us)
Async XLA Ops:
  2.0 17.3 %collective-permute-start.1 = (s32[9,96,2]{1,2,0:T(2,128)}, s32[9,96,2]{1,2,0:T(2,128)S(1)}, u32[]{:S(2)}, u32[]{:S(2)}) collective-permute-start(s32[9,96,2]{1,2,0:T(2,128)} %bitcast_select_fusion), channel_id=1, source_target_pairs={{2,0},{4,2},{6,4},{8,6},{10,8},{12,10},{14,12},{16,14},{18,16},{20... | collective-permute-start | bytes 20744 | tf_op jit(solution)/shard_map/ppermute | solution.py:17
  7.5 53.0 %collective-permute-start.4 = (s32[9,96,2]{1,2,0:T(2,128)}, s32[9,96,2]{1,2,0:T(2,128)}, u32[]{:S(2)}, u32[]{:S(2)}) collective-permute-start(s32[9,96,2]{1,2,0:T(2,128)} %bitcast_select_fusion), channel_id=1, source_target_pairs={{4,0},{6,2},{8,4},{10,6},{12,8},{14,10},{16,12},{18,14},{20,16},{2... | collective-permute-start | bytes 20744 | tf_op jit(solution)/shard_map/ppermute | solution.py:17
  13.9 17.8 %collective-permute-start.2 = (bf16[128,3072]{1,0:T(8,128)(2,1)S(1)}, bf16[128,3072]{1,0:T(8,128)(2,1)}, u32[]{:S(2)}, u32[]{:S(2)}) collective-permute-start(bf16[128,3072]{1,0:T(8,128)(2,1)S(1)} %reshape.119), channel_id=1, source_target_pairs={{2,0},{4,2},{6,4},{8,6},{10,8},{12,10},{14,12},{16,14},{18,16},{20... | collective-permute-start | bytes 2359304 | tf_op jit(solution)/shard_map/ppermute | solution.py:17
  14.3 21.2 %collective-permute-start = (bf16[128,3072]{1,0:T(8,128)(2,1)S(1)}, bf16[128,3072]{1,0:T(8,128)(2,1)}, u32[]{:S(2)}, u32[]{:S(2)}) collective-permute-start(bf16[128,3072]{1,0:T(8,128)(2,1)S(1)} %reshape.119), channel_id=1, source_target_pairs={{26,0},{28,2},{30,4},{0,6},{2,8},{4,10},{6,12},{8,14},{10,16},{12,... | collective-permute-start | bytes 2359304 | tf_op jit(solution)/shard_map/ppermute | solution.py:17
  33.2 4.3 %copy-start.4 = (bf16[96,3072]{1,0:T(8,128)(2,1)}, bf16[96,3072]{1,0:T(8,128)(2,1)S(1)}, u32[]{:S(2)}) copy-start(bf16[96,3072]{1,0:T(8,128)(2,1)S(1)} %fusion.454) | copy-start | bytes 1769476
  33.2 21.6 %slice-start = ((s8[8388608]{0:T(1024)(128)(4,1)}), s8[4194304]{0:T(1024)(128)(4,1)S(1)}, s32[]{:S(2)}) async-start(s8[8388608]{0:T(1024)(128)(4,1)} %bitcast.146), calls=%async_computation | async-start | bytes 8388608
  33.5 5.7 %copy-start.10 = (bf16[96,3072]{1,0:T(8,128)(2,1)S(1)}, bf16[96,3072]{1,0:T(8,128)(2,1)}, u32[]{:S(2)}) copy-start(bf16[96,3072]{1,0:T(8,128)(2,1)} %fusion.440) | copy-start | bytes 1769476
  35.5 1.9 %copy-start.8 = (bf16[96,3072]{1,0:T(8,128)(2,1)}, bf16[96,3072]{1,0:T(8,128)(2,1)S(1)}, u32[]{:S(2)}) copy-start(bf16[96,3072]{1,0:T(8,128)(2,1)S(1)} %fusion.455) | copy-start | bytes 1769476
  37.5 14.9 %copy-start.2 = (bf16[1024,2048]{1,0:T(8,128)(2,1)S(1)}, bf16[1024,2048]{1,0:T(8,128)(2,1)}, u32[]{:S(2)}) copy-start(bf16[1024,2048]{1,0:T(8,128)(2,1)} %constant.84) | copy-start | bytes 12582916
  40.5 13.0 %copy-start = (bf16[1024,2048]{1,0:T(8,128)(2,1)S(1)}, bf16[1024,2048]{1,0:T(8,128)(2,1)}, u32[]{:S(2)}) copy-start(bf16[1024,2048]{1,0:T(8,128)(2,1)} %constant.83) | copy-start | bytes 12582916
  40.5 11.9 %collective-permute-start.3 = (bf16[192,1024]{1,0:T(8,128)(2,1)S(1)}, bf16[192,1024]{1,0:T(8,128)(2,1)S(1)}, u32[]{:S(2)}, u32[]{:S(2)}) collective-permute-start(bf16[192,1024]{1,0:T(8,128)(2,1)S(1)} %fusion.54), channel_id=1, source_target_pairs={{1,0},{0,1},{3,2},{2,3},{5,4},{4,5},{7,6},{6,7},{9,8},{8,9},{11,10... | collective-permute-start | bytes 1179656 | tf_op jit(solution)/shard_map/ppermute | solution.py:17
  43.4 11.4 %slice-start.1 = ((s8[8388608]{0:T(1024)(128)(4,1)}), s8[4194304]{0:T(1024)(128)(4,1)S(1)}, s32[]{:S(2)}) async-start(s8[8388608]{0:T(1024)(128)(4,1)} %bitcast.146), calls=%async_computation.1 | async-start | bytes 8388608
  43.4 27.0 %collective-permute-start.7 = (bf16[128,3072]{1,0:T(8,128)(2,1)}, bf16[128,3072]{1,0:T(8,128)(2,1)}, u32[]{:S(2)}, u32[]{:S(2)}) collective-permute-start(bf16[128,3072]{1,0:T(8,128)(2,1)} %collective-permute-done.2), channel_id=1, source_target_pairs={{2,0},{4,2},{6,4},{8,6},{10,8},{12,10},{14,12},{16,14},{18,16},{20... | collective-permute-start | bytes 2359304 | tf_op jit(solution)/shard_map/ppermute | solution.py:17
  47.8 24.4 %collective-permute-start.6 = (bf16[128,3072]{1,0:T(8,128)(2,1)}, bf16[128,3072]{1,0:T(8,128)(2,1)}, u32[]{:S(2)}, u32[]{:S(2)}) collective-permute-start(bf16[128,3072]{1,0:T(8,128)(2,1)} %collective-permute-done), channel_id=1, source_target_pairs={{26,0},{28,2},{30,4},{0,6},{2,8},{4,10},{6,12},{8,14},{10,16},{12,... | collective-permute-start | bytes 2359304 | tf_op jit(solution)/shard_map/ppermute | solution.py:17
  64.4 16.6 %collective-permute-start.5 = (bf16[192,1024]{1,0:T(8,128)(2,1)S(1)}, bf16[192,1024]{1,0:T(8,128)(2,1)S(1)}, u32[]{:S(2)}, u32[]{:S(2)}) collective-permute-start(bf16[192,1024]{1,0:T(8,128)(2,1)S(1)} %fusion.50), channel_id=1, source_target_pairs={{1,0},{0,1},{3,2},{2,3},{5,4},{4,5},{7,6},{6,7},{9,8},{8,9},{11,10... | collective-permute-start | bytes 1179656 | tf_op jit(solution)/shard_map/ppermute | solution.py:17
  78.9 2.2 %copy-start.12 = (bf16[1,192,1024]{2,1,0:T(8,128)(2,1)S(1)}, bf16[1,192,1024]{2,1,0:T(8,128)(2,1)}, u32[]{:S(2)}) copy-start(bf16[1,192,1024]{2,1,0:T(8,128)(2,1)} %get-tuple-element.12) | copy-start | bytes 1179652
  81.4 3.6 %copy-start.9 = (bf16[96,3072]{1,0:T(8,128)(2,1)S(1)}, bf16[96,3072]{1,0:T(8,128)(2,1)}, u32[]{:S(2)}) copy-start(bf16[96,3072]{1,0:T(8,128)(2,1)} %copy-done.8) | copy-start | bytes 1769476
  81.7 13.3 %collective-permute-start.8 = (bf16[240,1024]{1,0:T(8,128)(2,1)S(1)}, bf16[240,1024]{1,0:T(8,128)(2,1)S(1)}, u32[]{:S(2)}, u32[]{:S(2)}) collective-permute-start(bf16[240,1024]{1,0:T(8,128)(2,1)S(1)} %fusion.35), channel_id=1, source_target_pairs={{1,0},{0,1},{3,2},{2,3},{5,4},{4,5},{7,6},{6,7},{9,8},{8,9},{11,10... | collective-permute-start | bytes 1474568 | tf_op jit(solution)/shard_map/ppermute | solution.py:17
  85.4 1.3 copy-start.7
  86.2 8.8 %copy-start.3 = (bf16[1024,2048]{1,0:T(8,128)(2,1)S(1)}, bf16[1024,2048]{1,0:T(8,128)(2,1)}, u32[]{:S(2)}) copy-start(bf16[1024,2048]{1,0:T(8,128)(2,1)} %constant.84) | copy-start | bytes 12582916
  88.9 7.5 %copy-start.1 = (bf16[1024,2048]{1,0:T(8,128)(2,1)S(1)}, bf16[1024,2048]{1,0:T(8,128)(2,1)}, u32[]{:S(2)}) copy-start(bf16[1024,2048]{1,0:T(8,128)(2,1)} %constant.83) | copy-start | bytes 12582916
  104.1 12.4 %collective-permute-start.9 = (bf16[240,1024]{1,0:T(8,128)(2,1)S(1)}, bf16[240,1024]{1,0:T(8,128)(2,1)S(1)}, u32[]{:S(2)}, u32[]{:S(2)}) collective-permute-start(bf16[240,1024]{1,0:T(8,128)(2,1)S(1)} %fusion.31), channel_id=1, source_target_pairs={{1,0},{0,1},{3,2},{2,3},{5,4},{4,5},{7,6},{6,7},{9,8},{8,9},{11,10... | collective-permute-start | bytes 1474568 | tf_op jit(solution)/shard_map/ppermute | solution.py:17
  119.9 19.9 %collective-permute-start.10 = (bf16[128,3072]{1,0:T(8,128)(2,1)S(1)}, bf16[128,3072]{1,0:T(8,128)(2,1)S(1)}, u32[]{:S(2)}, u32[]{:S(2)}) collective-permute-start(bf16[128,3072]{1,0:T(8,128)(2,1)S(1)} %convolution_convert_fusion.1), channel_id=1, source_target_pairs={{6,0},{8,2},{10,4},{12,6},{14,8},{16,10},{18,12},{20,14},{22,16},{... | collective-permute-start | bytes 2359304 | tf_op jit(solution)/shard_map/ppermute | solution.py:17
  122.1 17.7 %copy-start.16 = (bf16[96,3072]{1,0:T(8,128)(2,1)S(1)}, bf16[96,3072]{1,0:T(8,128)(2,1)}, u32[]{:S(2)}) copy-start(bf16[96,3072]{1,0:T(8,128)(2,1)} %copy-done.15) | copy-start | bytes 1769476
  122.1 17.7 %copy-start.19 = (pred[96,128]{1,0:T(32,128)(4,1)S(1)}, pred[96,128]{1,0:T(32,128)(4,1)}, u32[]{:S(2)}) copy-start(pred[96,128]{1,0:T(32,128)(4,1)} %iota_compare_fusion.17) | copy-start | bytes 36868
  122.1 17.7 %copy-start.22 = (pred[96,128]{1,0:T(32,128)(4,1)S(1)}, pred[96,128]{1,0:T(32,128)(4,1)}, u32[]{:S(2)}) copy-start(pred[96,128]{1,0:T(32,128)(4,1)} %iota_compare_fusion.12) | copy-start | bytes 36868
  122.7 18.9 %collective-permute-start.12 = (bf16[128,3072]{1,0:T(8,128)(2,1)S(1)}, bf16[128,3072]{1,0:T(8,128)(2,1)S(1)}, u32[]{:S(2)}, u32[]{:S(2)}) collective-permute-start(bf16[128,3072]{1,0:T(8,128)(2,1)S(1)} %convolution_convert_fusion), channel_id=1, source_target_pairs={{30,0},{0,2},{2,4},{4,6},{6,8},{8,10},{10,12},{12,14},{14,16},{16,... | collective-permute-start | bytes 2359304 | tf_op jit(solution)/shard_map/ppermute | solution.py:17
  122.9 18.7 %copy-start.18 = (bf16[96,3072]{1,0:T(8,128)(2,1)S(1)}, bf16[96,3072]{1,0:T(8,128)(2,1)}, u32[]{:S(2)}) copy-start(bf16[96,3072]{1,0:T(8,128)(2,1)} %copy-done.17) | copy-start | bytes 1769476
  122.9 18.7 %copy-start.20 = (pred[96,128]{1,0:T(32,128)(4,1)S(1)}, pred[96,128]{1,0:T(32,128)(4,1)}, u32[]{:S(2)}) copy-start(pred[96,128]{1,0:T(32,128)(4,1)} %iota_compare_fusion.13) | copy-start | bytes 36868
  122.9 18.7 %copy-start.21 = (pred[96,128]{1,0:T(32,128)(4,1)S(1)}, pred[96,128]{1,0:T(32,128)(4,1)}, u32[]{:S(2)}) copy-start(pred[96,128]{1,0:T(32,128)(4,1)} %iota_compare_fusion.16) | copy-start | bytes 36868
  141.5 19.9 %collective-permute-start.11 = (bf16[128,3072]{1,0:T(8,128)(2,1)S(1)}, bf16[128,3072]{1,0:T(8,128)(2,1)S(1)}, u32[]{:S(2)}, u32[]{:S(2)}) collective-permute-start(bf16[128,3072]{1,0:T(8,128)(2,1)S(1)} %add_convert_fusion.1), channel_id=1, source_target_pairs={{6,0},{8,2},{10,4},{12,6},{14,8},{16,10},{18,12},{20,14},{22,16},{... | collective-permute-start | bytes 2359304 | tf_op jit(solution)/shard_map/ppermute | solution.py:17
  142.3 19.2 %collective-permute-start.13 = (bf16[128,3072]{1,0:T(8,128)(2,1)S(1)}, bf16[128,3072]{1,0:T(8,128)(2,1)S(1)}, u32[]{:S(2)}, u32[]{:S(2)}) collective-permute-start(bf16[128,3072]{1,0:T(8,128)(2,1)S(1)} %add_convert_fusion), channel_id=1, source_target_pairs={{30,0},{0,2},{2,4},{4,6},{6,8},{8,10},{10,12},{12,14},{14,16},{16,... | collective-permute-start | bytes 2359304 | tf_op jit(solution)/shard_map/ppermute | solution.py:17
  (8 other events, 7.2 us)

commit v3 on v2

--- a/solution.py
+++ b/solution.py
@@ -99,15 +99,22 @@
         for behind in behinds:
             if ahead + behind < steps:
                 arrival = max(ahead, behind // reach, 1)
-                rounds.setdefault(arrival, []).append((ahead, behind))
+                later = arrival > 1 and ahead == arrival
+                rounds.setdefault((arrival, later), []).append((ahead, behind))
     after = jnp.int32(0)
-    for arrival in sorted(rounds):
-        active = rounds[arrival]
+    arrived = 1
+    for arrival, later in sorted(rounds):
+        active = rounds[(arrival, later)]
+        if arrival > arrived:
+            arrived = arrival
+            wait = after
+        elif arrival == 1:
+            wait = jnp.int32(0)
         picks = []
         rows = []
         crosses = []
         for ahead, behind in active:
-            chosen = lists_of[ahead][ahead + behind] + after
+            chosen = lists_of[ahead][ahead + behind] + wait
             pick_first = (chosen[:, 0:1] == station_ids[None, :]).astype(BF16)
             pick_second = (chosen[:, 1:2] == station_ids[None, :]).astype(BF16)
             a = planes(jnp.dot(pick_first, firsts[ahead], preferred_element_type=BF16))

time: 165 us -> 158 us (0.958)
  waiting for transfers between devices: 68.3 us -> 39 us
  starting transfers between devices: 17.1 us -> 32.9 us
  matrix products: 40.3 us -> 47.2 us
  other arithmetic: 27.3 us -> 25.1 us
  local copies, waits for them, and re-layouts: 9.04 us -> 11 us
    ppermute x14 -> x16, waiting for transfers between devices: 68.3 us -> 39 us  [from_behind(): return lax.ppermute(block, axis, route)]
    ppermute x14 -> x16, starting transfers between devices: 17.1 us -> 32.9 us  [from_behind(): return lax.ppermute(block, axis, route)]
    dot_general x2 -> x3, matrix products: 8.72 us -> 15.4 us  [on_device(): lax.dot_general(adjoint, table, (((1,), (1,)), ((), ())), preferred_eleme...]
    unnamed x52 -> x44, local copies, waits for them, and re-layouts: 3.09 us -> 5.08 us
    dot_general x4 -> x6, matrix products: 5.38 us -> 6.29 us  [on_device(): lagged = jnp.dot(full, table, preferred_element_type=F32)]
  transfers between devices with their start and end apart: 14 -> 16, of which waited for: 6 -> 8; matrix products, arithmetic and copies ran while one was open for 34% -> 44% of each run, Pallas kernels for 0% -> 0%
where the time goes in v3:
time: 158 us; the launch traced here: 157 us
  matrix products  47.2 us (30%)
  waiting for transfers between devices  39 us (25%)
  starting transfers between devices  32.9 us (21%)
  other arithmetic  25.1 us (16%)
  local copies, waits for them, and re-layouts  11 us (7%)
  between operations  1.7 us (1%)
    ppermute x16, waiting for transfers between devices, from_behind(): return lax.ppermute(block, axis, route)  39 us
    ppermute x16, starting transfers between devices, from_behind(): return lax.ppermute(block, axis, route)  32.9 us
    dot_general x3, matrix products, on_device(): lax.dot_general(adjoint, table, (((1,), (1,)), ((), ())), preferred_eleme...  15.4 us
    dot_general x9, matrix products, on_device(): a = planes(jnp.dot(pick_first, firsts[ahead], preferred_element_type=BF16))  11.1 us
    dot_general x9, matrix products, on_device(): jnp.dot(pick_second, seconds[behind], preferred_element_type=BF16)  10.2 us
    unnamed x91, other arithmetic  8.08 us
    dot_general x6, matrix products, on_device(): lagged = jnp.dot(full, table, preferred_element_type=F32)  6.29 us
    unnamed x44, local copies, waits for them, and re-layouts  5.08 us
  transfers between devices with their start and end apart: 16, of which 8 were waited for; matrix products, arithmetic and copies ran while one was open for 44% of the time, Pallas kernels for 0%

profile of v3, /device:TPU:0, one launch (start us, length us, event | category | flops | bytes accessed | tf_op | source)
XLA Modules:
  0.0 156.9 jit_solution(5083775964355666748)
XLA Ops:
  0.8 2.4 %fusion.22 = f32[128,512]{1,0:T(8,128)S(1)} fusion(bf16[128,3,2,512]{3,2,1,0:T(2,128)(2,1)} %param.5), kind=kLoop, calls=%fused_computation.36 | loop fusion | flops 1114112 | bytes 1048576 | tf_op jit(solution)/shard_map/reduce_sum | solution.py:33
  3.3 2.0 %fusion.23 = bf16[128,3,2,512]{3,2,1,0:T(2,128)(2,1)S(1)} fusion(bf16[128,3,2,512]{3,2,1,0:T(2,128)(2,1)} %param.5, f32[128,512]{1,0:T(8,128)S(1)} %rsqrt_select_fusion), kind=kLoop, calls=%fused_computation.37 | loop fusion | flops 1179648 | bytes 1835008 | tf_op jit(solution)/shard_map/convert_element_type | solution.py:36
  5.9 5.5 %collective-permute-start.2 = (bf16[128,3072]{1,0:T(8,128)(2,1)S(1)}, bf16[128,3072]{1,0:T(8,128)(2,1)}, u32[]{:S(2)}, u32[]{:S(2)}) collective-permute-start(bf16[128,3072]{1,0:T(8,128)(2,1)S(1)} %reshape.186), channel_id=1, source_target_pairs={{2,0},{4,2},{6,4},{8,6},{10,8},{12,10},{14,12},{16,14},{18,16},{20... | collective-permute-start | bytes 2359304 | tf_op jit(solution)/shard_map/ppermute | solution.py:17
  12.7 4.3 %collective-permute-start.4 = (s32[9,96,2]{1,2,0:T(2,128)}, s32[9,96,2]{1,2,0:T(2,128)}, u32[]{:S(2)}, u32[]{:S(2)}) collective-permute-start(s32[9,96,2]{1,2,0:T(2,128)} %bitcast_select_fusion.4), channel_id=1, source_target_pairs={{4,0},{6,2},{8,4},{10,6},{12,8},{14,10},{16,12},{18,14},{20,16},{2... | collective-permute-start | bytes 20744 | tf_op jit(solution)/shard_map/ppermute | solution.py:17
  22.1 5.3 %collective-permute-done.1 = s32[9,96,2]{1,2,0:T(2,128)S(1)} collective-permute-done((s32[9,96,2]{1,2,0:T(2,128)}, s32[9,96,2]{1,2,0:T(2,128)S(1)}, u32[]{:S(2)}, u32[]{:S(2)}) %collective-permute-start.1) | collective-permute-done | bytes 6944 | tf_op jit(solution)/shard_map/ppermute | solution.py:17
  28.5 2.1 %collective-permute-done = bf16[128,3072]{1,0:T(8,128)(2,1)} collective-permute-done((bf16[128,3072]{1,0:T(8,128)(2,1)S(1)}, bf16[128,3072]{1,0:T(8,128)(2,1)}, u32[]{:S(2)}, u32[]{:S(2)}) %collective-permute-start) | collective-permute-done | bytes 786464 | tf_op jit(solution)/shard_map/ppermute | solution.py:17
  32.1 1.6 %fusion.466 = bf16[96,3072]{1,0:T(8,128)(2,1)S(1)} fusion(bf16[128,3072]{1,0:T(8,128)(2,1)} %collective-permute-done.2, s32[96]{0:T(128)S(1)} %get-tuple-element.65), kind=kOutput, calls=%fused_computation.995 | convolution fusion | flops 75509760 | bytes 1376640 | tf_op jit(solution)/shard_map/dot_general | solution.py:120
  37.1 1.7 %fusion.464 = bf16[96,3072]{1,0:T(8,128)(2,1)S(1)} fusion(bf16[128,3072]{1,0:T(8,128)(2,1)} %collective-permute-done, s32[96]{0:T(128)S(1)} %get-tuple-element.70), kind=kOutput, calls=%fused_computation.993 | convolution fusion | flops 75509760 | bytes 1376640 | tf_op jit(solution)/shard_map/dot_general | solution.py:121
  40.0 1.6 collective-permute-start.3
  43.0 2.8 %collective-permute-start.9 = (bf16[128,3072]{1,0:T(8,128)(2,1)}, bf16[128,3072]{1,0:T(8,128)(2,1)}, u32[]{:S(2)}, u32[]{:S(2)}) collective-permute-start(bf16[128,3072]{1,0:T(8,128)(2,1)} %collective-permute-done.2), channel_id=1, source_target_pairs={{2,0},{4,2},{6,4},{8,6},{10,8},{12,10},{14,12},{16,14},{18,16},{20... | collective-permute-start | bytes 2359304 | tf_op jit(solution)/shard_map/ppermute | solution.py:17
  45.8 4.8 %collective-permute-done.3 = bf16[192,1024]{1,0:T(8,128)(2,1)S(1)} collective-permute-done((bf16[192,1024]{1,0:T(8,128)(2,1)S(1)}, bf16[192,1024]{1,0:T(8,128)(2,1)S(1)}, u32[]{:S(2)}, u32[]{:S(2)}) %collective-permute-start.3) | collective-permute-done | bytes 393248 | tf_op jit(solution)/shard_map/ppermute | solution.py:17
  53.1 2.9 %convolution_convert_fusion.2 = bf16[192,2048]{1,0:T(8,128)(2,1)S(1)} fusion(bf16[2048,2048]{1,0:T(8,128)(2,1)S(1)} %bitcast.179, f32[192,2048]{1,0:T(8,128)S(1)} %get-tuple-element.74, f32[192]{0:T(256)S(1)} %add_sqrt_fusion.1, f32[2048]{0:T(1024)S(1)} %multiply_add_fusion), kind=kOutput, calls=%fused_computation.4 | convolution fusion | flops 1612185600 | bytes 10756864 | tf_op jit(solution)/shard_map/dot_general | solution.py:135
  59.8 2.6 %collective-permute-start.5 = (bf16[192,1024]{1,0:T(8,128)(2,1)S(1)}, bf16[192,1024]{1,0:T(8,128)(2,1)S(1)}, u32[]{:S(2)}, u32[]{:S(2)}) collective-permute-start(bf16[192,1024]{1,0:T(8,128)(2,1)S(1)} %fusion.33), channel_id=1, source_target_pairs={{1,0},{0,1},{3,2},{2,3},{5,4},{4,5},{7,6},{6,7},{9,8},{8,9},{11,10... | collective-permute-start | bytes 1179656 | tf_op jit(solution)/shard_map/ppermute | solution.py:17
  65.5 1.5 fusion.469
  68.6 1.5 fusion.470
  70.4 1.5 fusion.468
  72.2 1.5 fusion.471
  81.4 2.1 %collective-permute-start.10 = (bf16[144,1024]{1,0:T(8,128)(2,1)S(1)}, bf16[144,1024]{1,0:T(8,128)(2,1)S(1)}, u32[]{:S(2)}, u32[]{:S(2)}) collective-permute-start(bf16[144,1024]{1,0:T(8,128)(2,1)S(1)} %fusion.47), channel_id=1, source_target_pairs={{1,0},{0,1},{3,2},{2,3},{5,4},{4,5},{7,6},{6,7},{9,8},{8,9},{11,10... | collective-permute-start | bytes 884744 | tf_op jit(solution)/shard_map/ppermute | solution.py:17
  84.3 1.5 copy-done.3
  88.4 6.1 %convolution_convert_fusion.4 = bf16[96,2048]{1,0:T(8,128)(2,1)S(1)} fusion(bf16[2048,2048]{1,0:T(8,128)(2,1)} %constant.97.clone, f32[96,2048]{1,0:T(8,128)S(1)} %get-tuple-element.78, f32[96]{0:T(128)S(1)} %add_sqrt_fusion.2, f32[2048]{0:T(1024)S(1)} %multiply_add_fusion), kind=kOutput, calls=%fused_computation.7 | convolution fusion | flops 806092800 | bytes 9576832 | tf_op jit(solution)/shard_map/dot_general | solution.py:135
  97.1 6.3 %convolution_convert_fusion.3 = bf16[144,2048]{1,0:T(8,128)(2,1)S(1)} fusion(bf16[2048,2048]{1,0:T(8,128)(2,1)} %constant.97.clone, f32[144,2048]{1,0:T(8,128)S(1)} %get-tuple-element.76, f32[144]{0:T(256)S(1)} %add_sqrt_fusion, f32[2048]{0:T(1024)S(1)} %multiply_add_fusion), kind=kOutput, calls=%fused_computation.5 | convolution fusion | flops 1209139200 | bytes 10166848 | tf_op jit(solution)/shard_map/dot_general | solution.py:135
  103.6 1.7 %collective-permute-start.11 = (bf16[144,1024]{1,0:T(8,128)(2,1)S(1)}, bf16[144,1024]{1,0:T(8,128)(2,1)S(1)}, u32[]{:S(2)}, u32[]{:S(2)}) collective-permute-start(bf16[144,1024]{1,0:T(8,128)(2,1)S(1)} %fusion.43), channel_id=1, source_target_pairs={{1,0},{0,1},{3,2},{2,3},{5,4},{4,5},{7,6},{6,7},{9,8},{8,9},{11,10... | collective-permute-start | bytes 884744 | tf_op jit(solution)/shard_map/ppermute | solution.py:17
  108.0 2.4 %collective-permute-done.11 = bf16[144,1024]{1,0:T(8,128)(2,1)S(1)} collective-permute-done((bf16[144,1024]{1,0:T(8,128)(2,1)S(1)}, bf16[144,1024]{1,0:T(8,128)(2,1)S(1)}, u32[]{:S(2)}, u32[]{:S(2)}) %collective-permute-start.11) | collective-permute-done | bytes 294944 | tf_op jit(solution)/shard_map/ppermute | solution.py:17
  114.2 4.3 %collective-permute-start.14 = (bf16[128,3072]{1,0:T(8,128)(2,1)S(1)}, bf16[128,3072]{1,0:T(8,128)(2,1)S(1)}, u32[]{:S(2)}, u32[]{:S(2)}) collective-permute-start(bf16[128,3072]{1,0:T(8,128)(2,1)S(1)} %convolution_convert_fusion), channel_id=1, source_target_pairs={{30,0},{0,2},{2,4},{4,6},{6,8},{8,10},{10,12},{12,14},{14,16},{16,... | collective-permute-start | bytes 2359304 | tf_op jit(solution)/shard_map/ppermute | solution.py:17
  118.6 7.8 %collective-permute-done.12 = bf16[128,3072]{1,0:T(8,128)(2,1)S(1)} collective-permute-done((bf16[128,3072]{1,0:T(8,128)(2,1)S(1)}, bf16[128,3072]{1,0:T(8,128)(2,1)S(1)}, u32[]{:S(2)}, u32[]{:S(2)}) %collective-permute-start.12) | collective-permute-done | bytes 786464 | tf_op jit(solution)/shard_map/ppermute | solution.py:17
  127.0 5.1 %collective-permute-start.13 = (bf16[128,3072]{1,0:T(8,128)(2,1)S(1)}, bf16[128,3072]{1,0:T(8,128)(2,1)S(1)}, u32[]{:S(2)}, u32[]{:S(2)}) collective-permute-start(bf16[128,3072]{1,0:T(8,128)(2,1)S(1)} %add_convert_fusion.1), channel_id=1, source_target_pairs={{6,0},{8,2},{10,4},{12,6},{14,8},{16,10},{18,12},{20,14},{22,16},{... | collective-permute-start | bytes 2359304 | tf_op jit(solution)/shard_map/ppermute | solution.py:17
  132.1 2.1 %collective-permute-done.14 = bf16[128,3072]{1,0:T(8,128)(2,1)S(1)} collective-permute-done((bf16[128,3072]{1,0:T(8,128)(2,1)S(1)}, bf16[128,3072]{1,0:T(8,128)(2,1)S(1)}, u32[]{:S(2)}, u32[]{:S(2)}) %collective-permute-start.14) | collective-permute-done | bytes 786464 | tf_op jit(solution)/shard_map/ppermute | solution.py:17
  134.8 1.7 %collective-permute-start.15 = (bf16[128,3072]{1,0:T(8,128)(2,1)S(1)}, bf16[128,3072]{1,0:T(8,128)(2,1)S(1)}, u32[]{:S(2)}, u32[]{:S(2)}) collective-permute-start(bf16[128,3072]{1,0:T(8,128)(2,1)S(1)} %add_convert_fusion), channel_id=1, source_target_pairs={{30,0},{0,2},{2,4},{4,6},{6,8},{8,10},{10,12},{12,14},{14,16},{16,... | collective-permute-start | bytes 2359304 | tf_op jit(solution)/shard_map/ppermute | solution.py:17
  137.9 1.7 %fusion.488 = f32[128,3072]{1,0:T(8,128)S(1)} fusion(pred[576,128]{1,0:T(8,128)(4,1)} %constant_dynamic-update-slice_fusion, bf16[576,3072]{1,0:T(8,128)(2,1)S(1)} %get-tuple-element.31), kind=kOutput, calls=%fused_computation.1013 | convolution fusion | flops 452984832 | bytes 5185536 | tf_op jit(solution)/shard_map/ps,pw->sw/dot_general | solution.py:161
  139.6 7.3 %collective-permute-done.13 = bf16[128,3072]{1,0:T(8,128)(2,1)S(1)} collective-permute-done((bf16[128,3072]{1,0:T(8,128)(2,1)S(1)}, bf16[128,3072]{1,0:T(8,128)(2,1)S(1)}, u32[]{:S(2)}, u32[]{:S(2)}) %collective-permute-start.13) | collective-permute-done | bytes 786464 | tf_op jit(solution)/shard_map/ppermute | solution.py:17
  146.9 7.2 %collective-permute-done.15 = bf16[128,3072]{1,0:T(8,128)(2,1)S(1)} collective-permute-done((bf16[128,3072]{1,0:T(8,128)(2,1)S(1)}, bf16[128,3072]{1,0:T(8,128)(2,1)S(1)}, u32[]{:S(2)}, u32[]{:S(2)}) %collective-permute-start.15) | collective-permute-done | bytes 786464 | tf_op jit(solution)/shard_map/ppermute | solution.py:17
  154.4 2.5 %reshape.187 = f32[128,3,2,512]{3,2,1,0:T(2,128)} reshape(f32[128,3072]{1,0:T(8,128)S(1)} %add_multiply_fusion) | data formatting | bytes 3145728 | tf_op jit(solution)/shard_map/reshape | solution.py:173
  (258 shorter events, 49.8 us)
Async XLA Ops:
  0.0 11.4 %copy-start.19 = (s32[1,9]{1,0:T(1,128)S(1)}, s32[1,9]{1,0:T(1,128)}, u32[]{:S(2)}) copy-start(s32[1,9]{1,0:T(1,128)} %param.8) | copy-start | bytes 112
  0.0 11.5 %copy-start.17 = (s32[1,9,96,2]{2,3,1,0:T(2,128)S(1)}, s32[1,9,96,2]{2,3,1,0:T(2,128)}, u32[]{:S(2)}) copy-start(s32[1,9,96,2]{2,3,1,0:T(2,128)} %param.7) | copy-start | bytes 20740
  5.9 26.2 %collective-permute-start.2 = (bf16[128,3072]{1,0:T(8,128)(2,1)S(1)}, bf16[128,3072]{1,0:T(8,128)(2,1)}, u32[]{:S(2)}, u32[]{:S(2)}) collective-permute-start(bf16[128,3072]{1,0:T(8,128)(2,1)S(1)} %reshape.186), channel_id=1, source_target_pairs={{2,0},{4,2},{6,4},{8,6},{10,8},{12,10},{14,12},{16,14},{18,16},{20... | collective-permute-start | bytes 2359304 | tf_op jit(solution)/shard_map/ppermute | solution.py:17
  11.4 19.2 %collective-permute-start = (bf16[128,3072]{1,0:T(8,128)(2,1)S(1)}, bf16[128,3072]{1,0:T(8,128)(2,1)}, u32[]{:S(2)}, u32[]{:S(2)}) collective-permute-start(bf16[128,3072]{1,0:T(8,128)(2,1)S(1)} %reshape.186), channel_id=1, source_target_pairs={{26,0},{28,2},{30,4},{0,6},{2,8},{4,10},{6,12},{8,14},{10,16},{12,... | collective-permute-start | bytes 2359304 | tf_op jit(solution)/shard_map/ppermute | solution.py:17
  12.1 15.3 %collective-permute-start.1 = (s32[9,96,2]{1,2,0:T(2,128)}, s32[9,96,2]{1,2,0:T(2,128)S(1)}, u32[]{:S(2)}, u32[]{:S(2)}) collective-permute-start(s32[9,96,2]{1,2,0:T(2,128)} %bitcast_select_fusion.4), channel_id=1, source_target_pairs={{2,0},{4,2},{6,4},{8,6},{10,8},{12,10},{14,12},{16,14},{18,16},{20... | collective-permute-start | bytes 20744 | tf_op jit(solution)/shard_map/ppermute | solution.py:17
  12.7 49.6 %collective-permute-start.4 = (s32[9,96,2]{1,2,0:T(2,128)}, s32[9,96,2]{1,2,0:T(2,128)}, u32[]{:S(2)}, u32[]{:S(2)}) collective-permute-start(s32[9,96,2]{1,2,0:T(2,128)} %bitcast_select_fusion.4), channel_id=1, source_target_pairs={{4,0},{6,2},{8,4},{10,6},{12,8},{14,10},{16,12},{18,14},{20,16},{2... | collective-permute-start | bytes 20744 | tf_op jit(solution)/shard_map/ppermute | solution.py:17
  27.4 24.3 %copy-start.18 = (s32[9,96,2]{1,2,0:T(2,128)}, s32[9,96,2]{1,2,0:T(2,128)S(1)}, u32[]{:S(2)}) copy-start(s32[9,96,2]{1,2,0:T(2,128)S(1)} %collective-permute-done.1) | copy-start | bytes 20740
  32.1 21.0 %slice-start = ((s8[8388608]{0:T(1024)(128)(4,1)}), s8[4194304]{0:T(1024)(128)(4,1)S(1)}, s32[]{:S(2)}) async-start(s8[8388608]{0:T(1024)(128)(4,1)} %bitcast.178), calls=%async_computation | async-start | bytes 8388608
  33.9 4.8 %copy-start.10 = (bf16[96,3072]{1,0:T(8,128)(2,1)S(1)}, bf16[96,3072]{1,0:T(8,128)(2,1)}, u32[]{:S(2)}) copy-start(bf16[96,3072]{1,0:T(8,128)(2,1)} %fusion.449) | copy-start | bytes 1769476
  37.1 13.6 %copy-start.2 = (bf16[1024,2048]{1,0:T(8,128)(2,1)S(1)}, bf16[1024,2048]{1,0:T(8,128)(2,1)}, u32[]{:S(2)}) copy-start(bf16[1024,2048]{1,0:T(8,128)(2,1)} %constant.101) | copy-start | bytes 12582916
  40.0 11.7 %copy-start = (bf16[1024,2048]{1,0:T(8,128)(2,1)S(1)}, bf16[1024,2048]{1,0:T(8,128)(2,1)}, u32[]{:S(2)}) copy-start(bf16[1024,2048]{1,0:T(8,128)(2,1)} %constant.100) | copy-start | bytes 12582916
  40.0 10.6 %collective-permute-start.3 = (bf16[192,1024]{1,0:T(8,128)(2,1)S(1)}, bf16[192,1024]{1,0:T(8,128)(2,1)S(1)}, u32[]{:S(2)}, u32[]{:S(2)}) collective-permute-start(bf16[192,1024]{1,0:T(8,128)(2,1)S(1)} %fusion.37), channel_id=1, source_target_pairs={{1,0},{0,1},{3,2},{2,3},{5,4},{4,5},{7,6},{6,7},{9,8},{8,9},{11,10... | collective-permute-start | bytes 1179656 | tf_op jit(solution)/shard_map/ppermute | solution.py:17
  43.0 10.1 %slice-start.1 = ((s8[8388608]{0:T(1024)(128)(4,1)}), s8[4194304]{0:T(1024)(128)(4,1)S(1)}, s32[]{:S(2)}) async-start(s8[8388608]{0:T(1024)(128)(4,1)} %bitcast.178), calls=%async_computation.1 | async-start | bytes 8388608
  43.0 25.6 %collective-permute-start.6 = (bf16[128,3072]{1,0:T(8,128)(2,1)}, bf16[128,3072]{1,0:T(8,128)(2,1)}, u32[]{:S(2)}, u32[]{:S(2)}) collective-permute-start(bf16[128,3072]{1,0:T(8,128)(2,1)} %collective-permute-done), channel_id=1, source_target_pairs={{26,0},{28,2},{30,4},{0,6},{2,8},{4,10},{6,12},{8,14},{10,16},{12,... | collective-permute-start | bytes 2359304 | tf_op jit(solution)/shard_map/ppermute | solution.py:17
  43.0 29.3 %collective-permute-start.9 = (bf16[128,3072]{1,0:T(8,128)(2,1)}, bf16[128,3072]{1,0:T(8,128)(2,1)}, u32[]{:S(2)}, u32[]{:S(2)}) collective-permute-start(bf16[128,3072]{1,0:T(8,128)(2,1)} %collective-permute-done.2), channel_id=1, source_target_pairs={{2,0},{4,2},{6,4},{8,6},{10,8},{12,10},{14,12},{16,14},{18,16},{20... | collective-permute-start | bytes 2359304 | tf_op jit(solution)/shard_map/ppermute | solution.py:17
  59.8 19.6 %collective-permute-start.5 = (bf16[192,1024]{1,0:T(8,128)(2,1)S(1)}, bf16[192,1024]{1,0:T(8,128)(2,1)S(1)}, u32[]{:S(2)}, u32[]{:S(2)}) collective-permute-start(bf16[192,1024]{1,0:T(8,128)(2,1)S(1)} %fusion.33), channel_id=1, source_target_pairs={{1,0},{0,1},{3,2},{2,3},{5,4},{4,5},{7,6},{6,7},{9,8},{8,9},{11,10... | collective-permute-start | bytes 1179656 | tf_op jit(solution)/shard_map/ppermute | solution.py:17
  75.9 3.5 %copy-start.12 = (bf16[1,192,1024]{2,1,0:T(8,128)(2,1)S(1)}, bf16[1,192,1024]{2,1,0:T(8,128)(2,1)}, u32[]{:S(2)}) copy-start(bf16[1,192,1024]{2,1,0:T(8,128)(2,1)} %get-tuple-element.10) | copy-start | bytes 1179652
  76.0 8.3 %collective-permute-start.7 = (bf16[96,1024]{1,0:T(8,128)(2,1)S(1)}, bf16[96,1024]{1,0:T(8,128)(2,1)S(1)}, u32[]{:S(2)}, u32[]{:S(2)}) collective-permute-start(bf16[96,1024]{1,0:T(8,128)(2,1)S(1)} %dynamic-slice_bitcast_fusion), channel_id=1, source_target_pairs={{1,0},{0,1},{3,2},{2,3},{5,4},{4,5},{7,6},{6,7},{9,8},{8,9},{11,10... | collective-permute-start | bytes 589832 | tf_op jit(solution)/shard_map/ppermute | solution.py:17
  80.9 2.7 %copy-start.7 = (bf16[96,3072]{1,0:T(8,128)(2,1)S(1)}, bf16[96,3072]{1,0:T(8,128)(2,1)}, u32[]{:S(2)}) copy-start(bf16[96,3072]{1,0:T(8,128)(2,1)} %copy-done.6) | copy-start | bytes 1769476
  81.4 13.7 %collective-permute-start.10 = (bf16[144,1024]{1,0:T(8,128)(2,1)S(1)}, bf16[144,1024]{1,0:T(8,128)(2,1)S(1)}, u32[]{:S(2)}, u32[]{:S(2)}) collective-permute-start(bf16[144,1024]{1,0:T(8,128)(2,1)S(1)} %fusion.47), channel_id=1, source_target_pairs={{1,0},{0,1},{3,2},{2,3},{5,4},{4,5},{7,6},{6,7},{9,8},{8,9},{11,10... | collective-permute-start | bytes 884744 | tf_op jit(solution)/shard_map/ppermute | solution.py:17
  83.6 2.2 %copy-start.3 = (bf16[1024,2048]{1,0:T(8,128)(2,1)S(1)}, bf16[1024,2048]{1,0:T(8,128)(2,1)}, u32[]{:S(2)}) copy-start(bf16[1024,2048]{1,0:T(8,128)(2,1)} %constant.101) | copy-start | bytes 12582916
  84.1 3.1 %copy-start.1 = (bf16[1024,2048]{1,0:T(8,128)(2,1)S(1)}, bf16[1024,2048]{1,0:T(8,128)(2,1)}, u32[]{:S(2)}) copy-start(bf16[1024,2048]{1,0:T(8,128)(2,1)} %constant.100) | copy-start | bytes 12582916
  94.7 10.6 %collective-permute-start.8 = (bf16[96,1024]{1,0:T(8,128)(2,1)S(1)}, bf16[96,1024]{1,0:T(8,128)(2,1)S(1)}, u32[]{:S(2)}, u32[]{:S(2)}) collective-permute-start(bf16[96,1024]{1,0:T(8,128)(2,1)S(1)} %fusion.380), channel_id=1, source_target_pairs={{1,0},{0,1},{3,2},{2,3},{5,4},{4,5},{7,6},{6,7},{9,8},{8,9},{11,10... | collective-permute-start | bytes 589832 | tf_op jit(solution)/shard_map/ppermute | solution.py:17
  103.6 6.8 %collective-permute-start.11 = (bf16[144,1024]{1,0:T(8,128)(2,1)S(1)}, bf16[144,1024]{1,0:T(8,128)(2,1)S(1)}, u32[]{:S(2)}, u32[]{:S(2)}) collective-permute-start(bf16[144,1024]{1,0:T(8,128)(2,1)S(1)} %fusion.43), channel_id=1, source_target_pairs={{1,0},{0,1},{3,2},{2,3},{5,4},{4,5},{7,6},{6,7},{9,8},{8,9},{11,10... | collective-permute-start | bytes 884744 | tf_op jit(solution)/shard_map/ppermute | solution.py:17
  111.7 14.6 %collective-permute-start.12 = (bf16[128,3072]{1,0:T(8,128)(2,1)S(1)}, bf16[128,3072]{1,0:T(8,128)(2,1)S(1)}, u32[]{:S(2)}, u32[]{:S(2)}) collective-permute-start(bf16[128,3072]{1,0:T(8,128)(2,1)S(1)} %convolution_convert_fusion.1), channel_id=1, source_target_pairs={{6,0},{8,2},{10,4},{12,6},{14,8},{16,10},{18,12},{20,14},{22,16},{... | collective-permute-start | bytes 2359304 | tf_op jit(solution)/shard_map/ppermute | solution.py:17
  113.5 12.9 %copy-start.13 = (pred[96,128]{1,0:T(32,128)(4,1)S(1)}, pred[96,128]{1,0:T(32,128)(4,1)}, u32[]{:S(2)}) copy-start(pred[96,128]{1,0:T(32,128)(4,1)} %iota_compare_fusion.17) | copy-start | bytes 36868
  113.5 12.9 %copy-start.14 = (pred[96,128]{1,0:T(32,128)(4,1)S(1)}, pred[96,128]{1,0:T(32,128)(4,1)}, u32[]{:S(2)}) copy-start(pred[96,128]{1,0:T(32,128)(4,1)} %iota_compare_fusion.12) | copy-start | bytes 36868
  114.2 20.0 %collective-permute-start.14 = (bf16[128,3072]{1,0:T(8,128)(2,1)S(1)}, bf16[128,3072]{1,0:T(8,128)(2,1)S(1)}, u32[]{:S(2)}, u32[]{:S(2)}) collective-permute-start(bf16[128,3072]{1,0:T(8,128)(2,1)S(1)} %convolution_convert_fusion), channel_id=1, source_target_pairs={{30,0},{0,2},{2,4},{4,6},{6,8},{8,10},{10,12},{12,14},{14,16},{16,... | collective-permute-start | bytes 2359304 | tf_op jit(solution)/shard_map/ppermute | solution.py:17
  118.6 15.6 %copy-start.15 = (pred[96,128]{1,0:T(32,128)(4,1)S(1)}, pred[96,128]{1,0:T(32,128)(4,1)}, u32[]{:S(2)}) copy-start(pred[96,128]{1,0:T(32,128)(4,1)} %iota_compare_fusion.13) | copy-start | bytes 36868
  118.6 15.6 %copy-start.16 = (pred[96,128]{1,0:T(32,128)(4,1)S(1)}, pred[96,128]{1,0:T(32,128)(4,1)}, u32[]{:S(2)}) copy-start(pred[96,128]{1,0:T(32,128)(4,1)} %iota_compare_fusion.16) | copy-start | bytes 36868
  127.0 19.9 %collective-permute-start.13 = (bf16[128,3072]{1,0:T(8,128)(2,1)S(1)}, bf16[128,3072]{1,0:T(8,128)(2,1)S(1)}, u32[]{:S(2)}, u32[]{:S(2)}) collective-permute-start(bf16[128,3072]{1,0:T(8,128)(2,1)S(1)} %add_convert_fusion.1), channel_id=1, source_target_pairs={{6,0},{8,2},{10,4},{12,6},{14,8},{16,10},{18,12},{20,14},{22,16},{... | collective-permute-start | bytes 2359304 | tf_op jit(solution)/shard_map/ppermute | solution.py:17
  134.8 19.3 %collective-permute-start.15 = (bf16[128,3072]{1,0:T(8,128)(2,1)S(1)}, bf16[128,3072]{1,0:T(8,128)(2,1)S(1)}, u32[]{:S(2)}, u32[]{:S(2)}) collective-permute-start(bf16[128,3072]{1,0:T(8,128)(2,1)S(1)} %add_convert_fusion), channel_id=1, source_target_pairs={{30,0},{0,2},{2,4},{4,6},{6,8},{8,10},{10,12},{12,14},{14,16},{16,... | collective-permute-start | bytes 2359304 | tf_op jit(solution)/shard_map/ppermute | solution.py:17
  (6 other events, 5.8 us)
